TPU v7x, 128 devices: a whole 4x4x4 slice. The times are simulated.
128 devices in a mesh: row: 16 (over x, y_hi, core), col: 8 (over y_lo, z).
Axes of the slice: x: 4, y: 4 (y_hi: 2, y_lo: 2; y = y_hi * 2 + y_lo), z: 4, core: 2. Of those that a mesh axis runs over, the one named last changes fastest.
Arguments:
- hamiltonian: bfloat16 [8192, 8192], P('row', 'col'), may hold values from -12 to 12, as said below
- density: bfloat16 [8192, 8192], P('row', 'col'), may hold values from -0.26516504 to 0.26516504, as said below
- h_flags: int32 [128, 128], P('row', 'col'), may hold values from 0 to 1, as said below
- p_flags: int32 [128, 128], P('row', 'col'), may hold values from 0 to 1, as said below
- q_flags: int32 [128, 128], P('row', 'col'), may hold values 0 or 1
- r_flags: int32 [128, 128], P('row', 'col'), may hold values 0 or 1
Outputs:
- gradient: float32 [8192, 8192], P(('row', 'col'))
Inputs may be any that keep to these rules, and one draw needn't show every extreme that they name: `h_flags`: symmetric; every diagonal block is occupied. `p_flags`: symmetric; every diagonal block is occupied. `hamiltonian`: symmetric. `density`: symmetric.
All inputs are finite; a program needn't handle non-finite values. No bound on the sum of `q_flags` or of `r_flags` on one device may be relied on, other than what follows from the above.
Results may differ from a plain program's by a relative error of at most 0.0029.
Values may be sent and summed in bfloat16 or wider, within the bound.
A program may use at most 128 MiB of HBM per device.

v0:
```python
import jax
import jax.numpy as jnp
from jax import lax
from jax.sharding import PartitionSpec as P

B = 64


def masked(matrix, flags):
    rows_blk, cols_blk = flags.shape
    shaped = matrix.reshape(rows_blk, B, cols_blk, B)
    return (shaped * flags.astype(matrix.dtype)[:, None, :, None]).reshape(matrix.shape)


def per_device(hamiltonian, density, h_flags, p_flags, q_flags, r_flags):
    h_masked = masked(hamiltonian, h_flags)
    p_masked = masked(density, p_flags)
    h_panel, p_panel = (
        lax.all_gather(h_masked, "col", axis=1, tiled=True),
        lax.all_gather(p_masked, "col", axis=1, tiled=True),
    )
    left = h_panel
    first_sum = jnp.dot(
        left,
        lax.all_gather(p_masked, "row", axis=0, tiled=True),
        preferred_element_type=jnp.float32,
    )
    first_tile = masked(first_sum, q_flags).astype(jnp.bfloat16)
    left = p_panel
    second_sum = jnp.dot(
        left,
        lax.all_gather(first_tile, "row", axis=0, tiled=True),
        preferred_element_type=jnp.float32,
    )
    second_tile = masked(second_sum, r_flags)
    first_line, second_line = (
        lax.all_to_all(
            first_tile.astype(jnp.float32), "col", split_axis=0, concat_axis=1, tiled=True
        ),
        lax.all_to_all(second_tile, "col", split_axis=0, concat_axis=1, tiled=True),
    )
    first_send = first_line.astype(jnp.bfloat16)
    own_part = first_line - 2.0 * second_line
    column_line = lax.all_to_all(
        first_send, ("row", "col"), split_axis=1, concat_axis=0, tiled=True
    )
    transposed = column_line.T.astype(jnp.float32)
    return own_part + transposed


def solution(mesh):
    return jax.shard_map(
        per_device,
        mesh=mesh,
        in_specs=(
            P("row", "col"),
            P("row", "col"),
            P("row", "col"),
            P("row", "col"),
            P("row", "col"),
            P("row", "col"),
        ),
        out_specs=P(("row", "col"), None),
        check_vma=False,
    )
```

profile of v0, /device:TPU:16, one launch (start us, length us, event | category | flops | bytes accessed | tf_op | source)
XLA Modules:
  0.0 544.3 jit_solution(2016372439834796426)
XLA Ops:
  7.6 1.5 mul.53
  9.1 2.6 mul.54
  13.6 2.6 mul.57
  17.1 2.4 mul.58
  19.5 3.5 mul.59
  23.0 82.9 %all-gather.5.cloned.1.call-done = bf16[512,8192]{1,0:T(8,128)(2,1)} async-done(((bf16[512,1024]{1,0:T(8,128)(2,1)}), bf16[512,8192]{1,0:T(8,128)(2,1)}) %all-gather.5.cloned.1.call-update) | async-done | bytes 8388624 | tf_op jit(solution)/shard_map/all_gather | solution.py:19
  105.9 109.1 %all-gather.7.cloned.1.call-done = bf16[8192,1024]{1,0:T(8,128)(2,1)} async-done(((bf16[512,1024]{1,0:T(8,128)(2,1)}), bf16[8192,1024]{1,0:T(8,128)(2,1)}) %all-gather.7.cloned.1.call-update) | async-done | bytes 16777232 | tf_op jit(solution)/shard_map/all_gather | solution.py:25
  215.0 15.6 %multiply_convert_fusion = bf16[512,1024]{1,0:T(8,128)(2,1)} fusion(f32[512,1024]{1,0:T(8,128)S(1)} %mul.59, bf16[512,8192]{1,0:T(8,128)(2,1)} %all-gather.5.cloned.1.call-done, bf16[8192,1024]{1,0:T(8,128)(2,1)} %all-gather.7.cloned.1.call-done), kind=kOutput, calls=%fused_computation.2 | convolution fusion | flops 8590983168 | bytes 28311552 | tf_op jit(solution)/shard_map/dot_general | solution.py:23
  230.6 2.3 mul.61
  232.9 5.0 mul.62
  237.9 1.6 convert.4
  239.5 6.0 %all-to-all-start = ((f32[8,64,1024]{2,1,0:T(8,128)}), f32[8,64,1024]{2,1,0:T(8,128)S(1)}, u32[]{:S(2)}, u32[]{:S(2)}) async-start(f32[8,64,1024]{2,1,0:T(8,128)} %convert.4), calls=%async_computation | async-start | bytes 4194304 | tf_op jit(solution)/shard_map/all_to_all | solution.py:37
  245.4 87.3 %all-gather.9.cloned.1.call-done = bf16[512,8192]{1,0:T(8,128)(2,1)} async-done(((bf16[512,1024]{1,0:T(8,128)(2,1)}), bf16[512,8192]{1,0:T(8,128)(2,1)}) %all-gather.9.cloned.1.call-update) | async-done | bytes 8388624 | tf_op jit(solution)/shard_map/all_gather | solution.py:20
  332.7 112.2 %all-gather.11.cloned.1.call-done = bf16[8192,1024]{1,0:T(8,128)(2,1)} async-done(((bf16[512,1024]{1,0:T(8,128)(2,1)}), bf16[8192,1024]{1,0:T(8,128)(2,1)}) %all-gather.11.cloned.1.call-update) | async-done | bytes 16777232 | tf_op jit(solution)/shard_map/all_gather | solution.py:32
  444.9 16.1 %convolution_multiply_fusion = f32[512,1024]{1,0:T(8,128)} fusion(f32[512,1024]{1,0:T(8,128)} %mul.62, bf16[512,8192]{1,0:T(8,128)(2,1)} %all-gather.9.cloned.1.call-done, bf16[8192,1024]{1,0:T(8,128)(2,1)} %all-gather.11.cloned.1.call-done), kind=kOutput, calls=%fused_computation.3 | convolution fusion | flops 8590458880 | bytes 29360128 | tf_op jit(solution)/shard_map/dot_general | solution.py:30
  461.0 33.2 %all_to_all.40 = f32[8,64,1024]{2,1,0:T(8,128)S(1)} all-to-all(f32[8,64,1024]{2,1,0:T(8,128)} %bitcast.35), channel_id=1, replica_groups=mesh['row'=16,'col'=8] {'col'}, dimensions={0} | all-to-all | bytes 4194304 | tf_op jit(solution)/shard_map/all_to_all | solution.py:40
  494.3 1.8 convert_bitcast_fusion
  498.0 2.7 copy.18
  500.7 4.8 reshape.35
  505.5 5.5 %all-to-all-start.2 = ((bf16[128,2,2048]{2,1,0:T(2,128)(2,1)}), bf16[128,2,2048]{2,1,0:T(2,128)(2,1)S(1)}, u32[]{:S(2)}, u32[]{:S(2)}) async-start(bf16[128,2,2048]{2,1,0:T(2,128)(2,1)} %reshape.35), calls=%async_computation.2 | async-start | bytes 2097152 | tf_op jit(solution)/shard_map/all_to_all | solution.py:44
  512.5 15.5 %all-to-all-done.2 = bf16[128,2,2048]{2,1,0:T(2,128)(2,1)S(1)} async-done(((bf16[128,2,2048]{2,1,0:T(2,128)(2,1)}), bf16[128,2,2048]{2,1,0:T(2,128)(2,1)S(1)}, u32[]{:S(2)}, u32[]{:S(2)}) %all-to-all-start.2) | async-done | bytes 1048608 | tf_op jit(solution)/shard_map/all_to_all | solution.py:44
  529.4 2.4 bitcast_convert_fusion
  531.8 2.8 copy.15
  534.6 3.1 bitcast_add_fusion
  (30 shorter events, 8.5 us)
Async XLA Ops:
  6.5 99.3 %all-gather.5.cloned.1.call-start = ((), (), s32[]{:S(2)}) async-start(), calls=%async_computation.3 | async-start | bytes 9437184 | tf_op jit(solution)/shard_map/all_gather | solution.py:19
  9.1 2.7 copy-start.2
  11.7 203.3 %all-gather.7.cloned.1.call-start = ((), (), s32[]{:S(2)}) async-start(), calls=%async_computation.4 | async-start | bytes 17825792 | tf_op jit(solution)/shard_map/all_gather | solution.py:25
  13.6 3.5 copy-start.3
  16.3 316.5 %all-gather.9.cloned.1.call-start = ((), (), s32[]{:S(2)}) async-start(), calls=%async_computation.5 | async-start | bytes 9437184 | tf_op jit(solution)/shard_map/all_gather | solution.py:20
  17.0 427.9 %all-gather.11.cloned.1.call-start = ((), (), s32[]{:S(2)}) async-start(), calls=%async_computation.6 | async-start | bytes 17825792 | tf_op jit(solution)/shard_map/all_gather | solution.py:32
  23.0 207.6 %copy-start.4 = (s32[8,16]{1,0:T(8,128)S(1)}, s32[8,16]{1,0:T(8,128)}, u32[]{:S(2)}) copy-start(s32[8,16]{1,0:T(8,128)} %param.11) | copy-start | bytes 1540
  232.9 5.0 copy-start.1
  239.5 221.5 %all-to-all-start = ((f32[8,64,1024]{2,1,0:T(8,128)}), f32[8,64,1024]{2,1,0:T(8,128)S(1)}, u32[]{:S(2)}, u32[]{:S(2)}) async-start(f32[8,64,1024]{2,1,0:T(8,128)} %convert.4), calls=%async_computation | async-start | bytes 4194304 | tf_op jit(solution)/shard_map/all_to_all | solution.py:37
  500.7 10.3 %copy-start = (f32[8,8,8,1024]{3,2,1,0:T(8,128)S(1)}, f32[8,8,8,1024]{3,2,1,0:T(8,128)}, u32[]{:S(2)}) copy-start(f32[8,8,8,1024]{3,2,1,0:T(8,128)} %get-tuple-element.6) | copy-start | bytes 6291460
  505.5 22.5 %all-to-all-start.2 = ((bf16[128,2,2048]{2,1,0:T(2,128)(2,1)}), bf16[128,2,2048]{2,1,0:T(2,128)(2,1)S(1)}, u32[]{:S(2)}, u32[]{:S(2)}) async-start(bf16[128,2,2048]{2,1,0:T(2,128)(2,1)} %reshape.35), calls=%async_computation.2 | async-start | bytes 2097152 | tf_op jit(solution)/shard_map/all_to_all | solution.py:44
Sparse Core Ops, SparseCore 0:
  11.8 93.9 all-gather.4
  108.3 106.6 all-gather.6
  216.6 116.0 all-gather.8
  335.0 109.8 all-gather.10
where the time goes:
time: 548 us; the launch traced here: 544 us
  waiting for transfers between devices  408 us (74%)
  blocking collectives  33.2 us (6%)
  local copies, waits for them, and re-layouts  31.9 us (6%)
  matrix products  31.7 us (6%)
  other arithmetic  14.9 us (3%)
  between operations  13.3 us (2%)
  starting transfers between devices  11.6 us (2%)
    all_gather x1, waiting for transfers between devices, per_device(): lax.all_gather(first_tile, 'row', axis=0, tiled=True)  112 us
    all_gather x1, waiting for transfers between devices, per_device(): lax.all_gather(p_masked, 'row', axis=0, tiled=True)  109 us
    all_gather x1, waiting for transfers between devices, per_device(): lax.all_gather(p_masked, 'col', axis=1, tiled=True)  87.3 us
    all_gather x1, waiting for transfers between devices, per_device(): lax.all_gather(h_masked, 'col', axis=1, tiled=True)  82.9 us
    all_to_all x1, blocking collectives, per_device(): lax.all_to_all(second_tile, 'col', split_axis=0, concat_axis=1, tiled=True)  33.2 us
    mul x8, local copies, waits for them, and re-layouts, masked(): shaped * flags.astype(matrix.dtype)[:, None, :, None]  16.8 us
    dot_general x1, matrix products, per_device(): jnp.dot(left, lax.all_gather(first_tile, 'row', axis=0, tiled=True), pref...  16.1 us
    dot_general x1, matrix products, per_device(): jnp.dot(left, lax.all_gather(p_masked, 'row', axis=0, tiled=True), prefer...  15.6 us
  transfers between devices with their start and end apart: 6, of which 5 were waited for; matrix products, arithmetic and copies ran while one was open for 10% of the time, Pallas kernels for 0%

commit v1 on v0

v1 whole, which is shorter than its diff:
```python
import functools

import jax
import jax.numpy as jnp
from jax import lax
from jax.experimental import pallas as pl
from jax.experimental.pallas import tpu as pltpu
from jax.sharding import PartitionSpec as P

MESH = pl.DeviceIdType.MESH
BF = jnp.bfloat16
F32 = jnp.float32
B = 64
T = 512


def dev(x, y, z, k):
    return (x * 4 + (y // 2) * 2 + k, (y % 2) * 4 + z)


def kernel(
    ham, den, flags, out,
    ps, hs, fs, pm, hm, acc, fb, ft, gs, qv, rv, qmask, rmask, rexp,
    p_send, p_recv, h_send, h_recv, f_send, f_recv, s_send, s_recv, o_send, o_recv,
):
    row, col = lax.axis_index("row"), lax.axis_index("col")
    x, yh, k = row // 4, (row // 2) % 2, row % 2
    yl, z = col // 4, col % 4
    y = yh * 2 + yl
    zh, zl = z // 2, z % 2
    me = x * 4 + y
    source_z = 2 * (x % 2) + yh

    def near(axis, step):
        if axis == "x":
            return dev((x + step) % 4, y, z, k)
        if axis == "y":
            return dev(x, (y + step) % 4, z, k)
        return dev(x, y, (z + step) % 4, k)

    core = dev(x, y, z, 1 - k)
    diagonal = dev(x, yh * 2 + 1 - yl, z, 1 - k)
    beside = dev(x, yh * 2 + 1 - yl, z, k)

    def remote(src, dst, send, recv, device):
        return pltpu.make_async_remote_copy(
            src_ref=src, dst_ref=dst, send_sem=send, recv_sem=recv,
            device_id=device, device_id_type=MESH,
        )

    barrier = pltpu.get_barrier_semaphore()

    def greet(device):
        pl.semaphore_signal(barrier, inc=1, device_id=device, device_id_type=MESH)

    for axis in "xyz":
        for step in (1, -1):
            greet(near(axis, step))
    greet(core)
    greet(diagonal)

    def scatter_source(j):
        return dev(2 * zl + 1 - zh, 2 * k + j, source_z, yl)

    for j in (0, 1):
        greet(scatter_source(j))
    on_way = (x % 2 == zh) & (yh == zl)

    def greet_out(g, carry):
        @pl.when(jnp.logical_not(on_way & (g == me)))
        def _():
            greet(dev(g // 4, g % 4, source_z, k))
        return carry

    lax.fori_loop(0, 16, greet_out, 0)

    def spread(first):
        blocks = lax.broadcasted_iota(jnp.int32, (128, T), 0)
        places = lax.broadcasted_iota(jnp.int32, (128, T), 1) // B
        return (blocks == places + first).astype(F32)

    for half in (0, 1):
        wide = spread(8 * half)
        h_wide = jnp.dot(flags[0], wide, preferred_element_type=F32)
        p_wide = jnp.dot(flags[1], wide, preferred_element_type=F32)
        for i in range(8):
            rows, columns = pl.ds(i * B, B), pl.ds(half * T, T)
            hm[rows, columns] = (ham[rows, columns].astype(F32) * h_wide[i : i + 1]).astype(BF)
            pm[half, rows, :] = (den[rows, columns].astype(F32) * p_wide[i : i + 1]).astype(BF)
    slot_q = 2 * k + yl
    qv[slot_q] = flags[2]
    acc[...] = jnp.zeros_like(acc)

    pl.semaphore_wait(barrier, 26 - on_way.astype(jnp.int32))

    pending = []

    def go(copy):
        copy.start()
        pending.append(copy)

    p_own = pltpu.make_async_copy(pm.at[k], ps.at[me, pl.ds(k * T, T)], p_recv.at[40])
    p_own.start()
    p_swap = remote(pm.at[1 - k], ps.at[me, pl.ds(k * T, T)], p_send.at[41], p_recv.at[41], core)
    go(p_swap)

    @pl.when(k == yl)
    def _():
        pltpu.make_async_copy(hm, hs.at[4 * k + z], h_recv.at[8]).start()

    h_swap = remote(hm, hs.at[4 * (1 - k) + z], h_send.at[8], h_recv.at[8], diagonal)

    @pl.when(k != yl)
    def _():
        h_swap.start()

    go(remote(qv.at[slot_q], qv.at[slot_q], s_send.at[0], s_recv.at[0], core))
    go(remote(qv.at[slot_q], qv.at[slot_q], s_send.at[1], s_recv.at[1], diagonal))
    go(remote(qv.at[slot_q], qv.at[slot_q], s_send.at[2], s_recv.at[2], beside))
    r_local = []
    for side in (0, 1):
        tx, ty, tz = 2 * yl + zh, 2 * zl + side, source_z
        own = (tx == x) & (ty == y) & (tz == z)
        copy = remote(flags.at[3], rv.at[x // 2], s_send.at[3 + side], s_recv.at[3 + x // 2], dev(tx, ty, tz, k))
        pl.when(jnp.logical_not(own))(copy.start)
        local = pltpu.make_async_copy(flags.at[3], rv.at[x // 2], s_recv.at[3 + x // 2])
        pl.when(own)(local.start)
        r_local.append((own, copy))

    def got(dst, recv):
        remote(dst, dst, s_send.at[0], recv, core).wait_recv()

    def slot(dx, dy):
        return ((x + dx) % 4) * 4 + (y + dy) % 4

    def place(h, a, b):
        return slot(a, b) if h == 0 else slot(b, a)

    def p_part(h, a, b, part):
        first, size = (h * T, T) if part is None else (h * T + part * 256, 256)
        return ps.at[place(h, a, b), pl.ds(first, size)]

    def p_go(h, a, b, part, axis, step, index):
        ref = p_part(h, a, b, part)
        go(remote(ref, ref, p_send.at[index], p_recv.at[index], near(axis, step)))

    def p_got(h, a, b, part, index):
        got(p_part(h, a, b, part), p_recv.at[index])

    AXES = (("x", "y"), ("y", "x"))
    OFFSET = (0, -1, 1, 2)

    def first_start(h):
        p_go(h, 0, 0, None, AXES[h][0], 1, 20 * h)
        p_go(h, 0, 0, None, AXES[h][0], -1, 20 * h + 1)

    def first_pass(h):
        p_got(h, -1, 0, None, 20 * h)
        p_go(h, -1, 0, 0, AXES[h][0], 1, 20 * h + 2)
        p_got(h, 1, 0, None, 20 * h + 1)
        p_go(h, 1, 0, 1, AXES[h][0], -1, 20 * h + 3)

    def first_end(h):
        p_got(h, 2, 0, 0, 20 * h + 2)
        p_got(h, 2, 0, 1, 20 * h + 3)

    def second_start(h, j):
        base = 20 * h + 4 + 4 * j
        p_go(h, OFFSET[j], 0, None, AXES[h][1], 1, base)
        p_go(h, OFFSET[j], 0, None, AXES[h][1], -1, base + 1)

    def second_pass(h, j):
        base = 20 * h + 4 + 4 * j
        p_got(h, OFFSET[j], -1, None, base)
        p_go(h, OFFSET[j], -1, 0, AXES[h][1], 1, base + 2)
        p_got(h, OFFSET[j], 1, None, base + 1)
        p_go(h, OFFSET[j], 1, 1, AXES[h][1], -1, base + 3)

    def second_end(h, j):
        base = 20 * h + 4 + 4 * j
        p_got(h, OFFSET[j], 2, 0, base + 2)
        p_got(h, OFFSET[j], 2, 1, base + 3)

    def multiply(places):
        def add(dx, dy):
            s = slot(dx, dy)
            acc[s % 2] += jnp.dot(hs[s // 2], ps[s], preferred_element_type=F32)

        if len(places) == 1:
            add(*places[0])
            return

        def body(n, carry):
            dx = sum(jnp.where(n == i, p[0], 0) for i, p in enumerate(places))
            dy = sum(jnp.where(n == i, p[1], 0) for i, p in enumerate(places))
            add(dx, dy)
            return carry

        lax.fori_loop(0, len(places), body, 0)

    p_own.wait()
    got(ps.at[me, pl.ds((1 - k) * T, T)], p_recv.at[41])
    for h in (0, 1):
        first_start(h)
    for h in (0, 1):
        second_start(h, 0)

    h_home = 4 * k + z
    got(hs.at[h_home], h_recv.at[8])

    def h_slot(step, c):
        return 4 * c + (z + step) % 4

    def h_go(step, part, way, index):
        ref = hs.at[h_slot(step, k)] if part is None else hs.at[h_slot(step, k), pl.ds(part * 256, 256)]
        go(remote(ref, ref, h_send.at[index], h_recv.at[index], near("z", way)))

    def h_got(step, part, index):
        ref = hs.at[h_slot(step, k)] if part is None else hs.at[h_slot(step, k), pl.ds(part * 256, 256)]
        got(ref, h_recv.at[index])

    def h_share(step, index):
        ref = hs.at[h_slot(step, k)]
        go(remote(ref, ref, h_send.at[index], h_recv.at[index], core))

    h_go(0, None, 1, 0)
    h_go(0, None, -1, 1)
    h_share(0, 4)

    for h in (0, 1):
        first_pass(h)
        second_start(h, 1)
        second_start(h, 2)
    for n, place_q in enumerate((2 * (1 - k) + yl, 2 * (1 - k) + 1 - yl, 2 * k + 1 - yl)):
        got(qv.at[place_q], s_recv.at[n])
    for n in range(2):
        got(rv.at[n], s_recv.at[3 + n])
    narrow = spread(8 * k)
    for c in (0, 1):
        q_wide = jnp.dot(qv[2 * yl + c], narrow, preferred_element_type=F32)
        for i in range(8):
            qmask[c, pl.ds(i * B, B), :] = jnp.broadcast_to(q_wide[i : i + 1], (B, T)).astype(BF)
        eight = (lax.broadcasted_iota(jnp.int32, (8, T), 0) == lax.broadcasted_iota(jnp.int32, (8, T), 1) // B)
        rexp[...] = lax.dot_general(rv[c], eight.astype(F32), (((0,), (0,)), ((), ())), preferred_element_type=F32)
        r_wide = rexp[pl.ds(pl.multiple_of(yl * 8, 8), 8), :]
        for i in range(8):
            rmask[c, pl.ds(i * B, B), :] = jnp.broadcast_to(2.0 * r_wide[i : i + 1], (B, T)).astype(BF)

    for h in (0, 1):
        second_pass(h, 0)
    h_got(-1, None, 0)
    h_go(-1, 0, 1, 2)
    h_share(-1, 5)
    h_got(1, None, 1)
    h_go(1, 1, -1, 3)
    h_share(1, 6)
    for h in (0, 1):
        first_end(h)
        second_start(h, 3)
    for h in (0, 1):
        second_end(h, 0)
    h_got(2, 0, 2)
    h_got(2, 1, 3)
    h_share(2, 7)
    for h in (0, 1):
        second_pass(h, 1)
        second_pass(h, 2)
    for n, step in enumerate((0, -1, 1, 2)):
        got(hs.at[h_slot(step, 1 - k)], h_recv.at[4 + n])
    multiply([(0, 0), (1, 0), (-1, 0), (0, 1), (0, -1), (2, 0), (0, 2), (1, 1), (1, -1), (-1, 1), (-1, -1)])
    for h in (0, 1):
        second_pass(h, 3)
    for h in (0, 1):
        second_end(h, 1)
        second_end(h, 2)
    multiply([(2, 1), (2, -1), (1, 2), (-1, 2)])
    for h in (0, 1):
        second_end(h, 3)
    multiply([(2, 2)])

    for c in (0, 1):
        first = acc[c] * qmask[c].astype(F32)
        fb[c] = first.astype(BF)
        ft[c] = first.T.astype(BF)
        target = dev(2 * c + zh, 2 * zl + k, 2 * (1 - x % 2) + x // 2, yh)
        go(remote(ft.at[c], fs.at[me], f_send.at[c], f_recv.at[yl], target))
        acc[c] = jnp.zeros((T, T), F32)

    def f_slot(step, c, j):
        zz = (z + step) % 4
        return (2 * (zz % 2) + 1 - zz // 2) * 4 + 2 * c + j

    def f_go(step, j, device, index):
        ref = fs.at[f_slot(step, k, j)]
        go(remote(ref, ref, f_send.at[index], f_recv.at[index], device))

    def f_got(step, c, j, index):
        got(fs.at[f_slot(step, c, j)], f_recv.at[index])

    def multiply_second(n, fn):
        def body(i, carry):
            step, c = fn(i)
            zz = (z + step) % 4
            xs = 2 * (zz % 2) + 1 - zz // 2
            for j in (0, 1):
                for half in (0, 1):
                    acc[half] += jnp.dot(
                        fs[xs * 4 + 2 * c + j], ps[xs * 4 + 2 * c + half, pl.ds(j * T, T), :],
                        preferred_element_type=F32,
                    )
            return carry

        lax.fori_loop(0, n, body, 0)

    for j in (0, 1):
        f_got(0, k, j, j)
        f_go(0, j, near("z", 1), 2 + j)
        f_go(0, j, near("z", -1), 4 + j)
        f_go(0, j, core, 8 + j)
    multiply_second(1, lambda i: (0, k))
    for j in (0, 1):
        f_got(-1, k, j, 2 + j)
        if j == 0:
            f_go(-1, 0, near("z", 1), 6)
        f_go(-1, j, core, 10 + j)
        f_got(1, k, j, 4 + j)
        if j == 1:
            f_go(1, 1, near("z", -1), 7)
        f_go(1, j, core, 12 + j)
    for j in (0, 1):
        f_got(0, 1 - k, j, 8 + j)
    multiply_second(3, lambda i: (jnp.where(i == 0, 0, 2 * i - 3), jnp.where(i == 0, 1 - k, k)))
    for j in (0, 1):
        f_got(2, k, j, 6 + j)
        f_go(2, j, core, 14 + j)
    for j in (0, 1):
        f_got(-1, 1 - k, j, 10 + j)
        f_got(1, 1 - k, j, 12 + j)
    multiply_second(3, lambda i: (jnp.where(i == 0, 2, 2 * i - 3), jnp.where(i == 0, k, 1 - k)))
    for j in (0, 1):
        f_got(2, 1 - k, j, 14 + j)
    multiply_second(1, lambda i: (2, 1 - k))

    o_copies = []
    for c in (0, 1):
        turned = fs[(2 * c + zh) * 4 + 2 * zl + k].astype(F32)
        value = fb[c].astype(F32) + turned - acc[c] * rmask[c].astype(F32)
        gs[c] = value.T.astype(BF)
        mine = pl.ds(pl.multiple_of(me * T, T), T)

        def send_rows(b, carry, wait=False, c=c):
            rows = gs.at[c, pl.ds(pl.multiple_of(b * B, B), B)]
            tx, ty, tz = 2 * c + zh, 2 * zl + b // 4, b % 4
            own = (tx == x) & (ty == y) & (tz == z)
            copy = remote(rows, out.at[:, mine], o_send.at[c * 8 + b], o_recv.at[me], dev(tx, ty, tz, k))
            pl.when(jnp.logical_not(own))(copy.wait_send if wait else copy.start)
            if not wait:
                pl.when(own)(pltpu.make_async_copy(rows, out.at[:, mine], o_recv.at[me]).start)
            return carry

        lax.fori_loop(0, 8, send_rows, 0)
        o_copies.append(functools.partial(send_rows, wait=True))

    def take(g, carry):
        got(out.at[:, pl.ds(pl.multiple_of(g * T, T), T)], o_recv.at[g])
        return carry

    lax.fori_loop(0, 16, take, 0)
    for copy in pending:
        copy.wait_send()
    pl.when(k != yl)(h_swap.wait_send)
    for own, copy in r_local:
        pl.when(jnp.logical_not(own))(copy.wait_send)
    for wait in o_copies:
        lax.fori_loop(0, 8, wait, 0)


def per_device(hamiltonian, density, h_flags, p_flags, q_flags, r_flags):
    flags = jnp.stack([h_flags, p_flags, q_flags, r_flags]).astype(F32)
    flags = jnp.pad(flags, ((0, 0), (0, 0), (0, 112)))
    dma = pltpu.SemaphoreType.DMA
    rows = pl.pallas_call(
        kernel,
        out_shape=jax.ShapeDtypeStruct((64, 8192), BF),
        in_specs=[pl.BlockSpec(memory_space=pltpu.VMEM)] * 3,
        out_specs=pl.BlockSpec(memory_space=pl.ANY),
        scratch_shapes=[
            pltpu.VMEM((16, 2 * T, T), BF),
            pltpu.VMEM((8, T, 2 * T), BF),
            pltpu.VMEM((16, T, T), BF),
            pltpu.VMEM((2, T, T), BF),
            pltpu.VMEM((T, 2 * T), BF),
            pltpu.VMEM((2, T, T), F32),
            pltpu.VMEM((2, T, T), BF),
            pltpu.VMEM((2, T, T), BF),
            pltpu.VMEM((2, T, T), BF),
            pltpu.VMEM((4, 8, 128), F32),
            pltpu.VMEM((2, 8, 128), F32),
            pltpu.VMEM((2, T, T), BF),
            pltpu.VMEM((2, T, T), BF),
            pltpu.VMEM((128, T), F32),
            dma((42,)), dma((42,)), dma((9,)), dma((9,)), dma((16,)), dma((16,)),
            dma((5,)), dma((5,)), dma((16,)), dma((16,)),
        ],
        compiler_params=pltpu.CompilerParams(
            collective_id=0, has_side_effects=True, vmem_limit_bytes=60 * 1024 * 1024
        ),
        cost_estimate=pl.CostEstimate(flops=2 * 2 * 512 * 8192 * 1024, bytes_accessed=4 << 20, transcendentals=0),
    )(hamiltonian, density, flags)
    return rows.astype(F32)


def solution(mesh):
    spec = P("row", "col")
    return jax.shard_map(
        per_device,
        mesh=mesh,
        in_specs=(spec,) * 6,
        out_specs=P(("row", "col"), None),
        check_vma=False,
    )
```

time: 548 us -> 254 us (0.46)
  waiting for transfers between devices: 408 us -> 0 us
  Pallas kernels: 0 us -> 248 us
  blocking collectives: 33.2 us -> 0 us
  matrix products: 31.7 us -> 0 us
  local copies, waits for them, and re-layouts: 31.9 us -> 0.61 us
  between operations: 13.3 us -> 0.01 us
  starting transfers between devices: 11.6 us -> 0 us
  other arithmetic: 14.9 us -> 3.42 us
    all_gather x4 -> x0, waiting for transfers between devices: 391 us -> none  [the longest x1 112 us: per_device(): lax.all_gather(first_tile, 'row', axis=0, tiled=True)]
    pallas_call x0 -> x1, Pallas kernels: none -> 248 us  [per_device(): pl.pallas_call(kernel, out_shape=jax.ShapeDtypeStruct((64, 8192), BF), in...]
    all_to_all x1 -> x0, blocking collectives: 33.2 us -> none  [per_device(): lax.all_to_all(second_tile, 'col', split_axis=0, concat_axis=1, tiled=True)]
    dot_general x2 -> x0, matrix products: 31.7 us -> none  [the longest x1 16.1 us: per_device(): jnp.dot(left, lax.all_gather(first_tile, 'row', axis=0, tiled=True), pref...]
    mul x8 -> x0, local copies, waits for them, and re-layouts: 16.8 us -> none  [masked(): shaped * flags.astype(matrix.dtype)[:, None, :, None]]
    all_to_all x2 -> x0, waiting for transfers between devices: 15.5 us -> none  [the longest x1 15.5 us: per_device(): lax.all_to_all(first_send, ('row', 'col'), split_axis=1, concat_axis=0, t...]
    all_to_all x2 -> x0, starting transfers between devices: 11.5 us -> none  [the longest x1 5.95 us: per_device(): lax.all_to_all(first_tile.astype(jnp.float32), 'col', split_axis=0, conca...]
    convert_element_type x4 -> x0, local copies, waits for them, and re-layouts: 7.43 us -> none  [the longest x3 4.61 us: per_device(): first_send = first_line.astype(jnp.bfloat16)]
  transfers between devices with their start and end apart: 6 -> 0, of which waited for: 5 -> 0; matrix products, arithmetic and copies ran while one was open for 10% -> 0% of each run, Pallas kernels for 0% -> 0%
where the time goes in v1:
time: 254 us; the launch traced here: 252 us
  Pallas kernels  248 us (98%)
  other arithmetic  3.42 us (1%)
    pallas_call x1, Pallas kernels, per_device(): pl.pallas_call(kernel, out_shape=jax.ShapeDtypeStruct((64, 8192), BF), in...  248 us

profile of v1, /device:TPU:16, one launch (start us, length us, event | category | flops | bytes accessed | tf_op | source)
XLA Modules:
  0.0 252.2 jit_solution(17592341395308043635)
XLA Ops:
  0.0 0.7 add_convert_fusion
  0.7 0.6 pad.4.flags
  1.4 248.2 %shard_map.64 = bf16[64,8192]{1,0:T(8,128)(2,1)} custom-call(bf16[512,1024]{1,0:T(8,128)(2,1)} %ham.1, bf16[512,1024]{1,0:T(8,128)(2,1)} %den.1, f32[4,8,128]{2,1,0:T(8,128)} %pad.4.flags), custom_call_target="tpu_custom_call" | custom-call | flops 17179869184 | bytes 4194304 | tf_op jit(solution)/shard_map/pallas_call | solution.py:382
  249.5 2.7 %convert_element_type.9 = f32[64,8192]{1,0:T(8,128)} convert(bf16[64,8192]{1,0:T(8,128)(2,1)} %shard_map.64) | non-fusion elementwise | flops 524288 | bytes 3145728 | tf_op jit(solution)/shard_map/convert_element_type | solution.py:410

commit v2 on v0

v2 whole, which is shorter than its diff:
```python
import jax
import jax.numpy as jnp
from jax import lax
from jax.experimental import pallas as pl
from jax.experimental.pallas import tpu as pltpu
from jax.sharding import PartitionSpec as P

MESH = pl.DeviceIdType.MESH
BF = jnp.bfloat16
F32 = jnp.float32
B = 64
T = 512
U = 256


def dev(x, y, z, k):
    return (x * 4 + (y // 2) * 2 + k, (y % 2) * 4 + z)


def kernel(
    ham, den, flags, out,
    ps, hs, fs, hm, acc, sums, fb, ft, gs, qv, rv, qmask, rmask, qexp,
    p_send, p_recv, h_send, h_recv, f_send, f_recv, s_send, s_recv, o_send, o_recv,
):
    row, col = lax.axis_index("row"), lax.axis_index("col")
    x, yh, k = row // 4, (row // 2) % 2, row % 2
    yl, z = col // 4, col % 4
    y = yh * 2 + yl
    zh, zl = z // 2, z % 2
    xh, xl = x // 2, x % 2
    me = y * 4 + z
    plane = 2 * yl + zh

    def near(axis, step):
        if axis == "x":
            return dev((x + step) % 4, y, z, k)
        if axis == "y":
            return dev(x, (y + step) % 4, z, k)
        return dev(x, y, (z + step) % 4, k)

    core = dev(x, y, z, 1 - k)
    across = near("y", 2)

    def remote(src, dst, send, recv, device):
        return pltpu.make_async_remote_copy(
            src_ref=src, dst_ref=dst, send_sem=send, recv_sem=recv,
            device_id=device, device_id_type=MESH,
        )

    barrier = pltpu.get_barrier_semaphore()

    def greet(device):
        pl.semaphore_signal(barrier, inc=1, device_id=device, device_id_type=MESH)

    def greet_plane(n, carry):
        greet(dev(x, (y + n // 4) % 4, (z + n % 4) % 4, k))
        return carry

    lax.fori_loop(1, 16, greet_plane, 0)
    greet(near("x", 1))
    greet(near("x", -1))
    greet(core)
    for j in (0, 1):
        greet(dev(plane, (x + plane) % 4, 2 * (1 - k) + j, yh))
    mirror = (x == plane) & (y == 2 * k + xh) & (z == 2 * xl + yh)
    for c in (0, 1):
        pl.when(jnp.logical_not(mirror & (zl == c)))(
            lambda c=c: greet(dev(plane, 2 * zl + xh, 2 * xl + c, yh))
        )

    def spread(first):
        blocks = lax.broadcasted_iota(jnp.int32, (128, T), 0)
        places = lax.broadcasted_iota(jnp.int32, (128, T), 1) // B
        return (blocks == places + first).astype(F32)

    for half in (0, 1):
        wide = spread(8 * half)
        h_wide = jnp.dot(flags[0], wide, preferred_element_type=F32)
        p_wide = jnp.dot(flags[1], wide, preferred_element_type=F32)
        for i in range(8):
            rows, columns = pl.ds(i * B, B), pl.ds(half * T, T)
            ps[me, half, rows, :] = (den[rows, columns].astype(F32) * p_wide[i : i + 1]).astype(BF)
            hm[half, rows, :] = (ham[rows, columns].astype(F32) * h_wide[i : i + 1]).astype(BF)
    rv[yh] = flags[3]

    pl.semaphore_wait(barrier, 22 - mirror.astype(jnp.int32))

    pending = []

    def go(copy):
        copy.start()
        pending.append(copy)

    def got(dst, recv):
        remote(dst, dst, s_send.at[0], recv, core).wait_recv()

    AXES = (("y", "z"), ("z", "y"))
    OFFSET = (0, -1, 1, 2)

    def p_part(u, h, a, b, part):
        dy, dz = (a, b) if h == 0 else (b, a)
        s = ((y + dy) % 4) * 4 + (z + dz) % 4
        first, size = (u * U + h * 128, 128) if part is None else (u * U + h * 128 + part * 64, 64)
        return ps.at[s, :, pl.ds(first, size), :]

    def p_go(u, h, a, b, part, axis, step, index):
        ref = p_part(u, h, a, b, part)
        go(remote(ref, ref, p_send.at[index], p_recv.at[index], near(axis, step)))

    def p_got(u, h, a, b, part, index):
        got(p_part(u, h, a, b, part), p_recv.at[index])

    def first_start(u):
        for h in (0, 1):
            base = 40 * u + 20 * h
            p_go(u, h, 0, 0, None, AXES[h][0], 1, base)
            p_go(u, h, 0, 0, None, AXES[h][0], -1, base + 1)

    def first_pass(u):
        for h in (0, 1):
            base = 40 * u + 20 * h
            p_got(u, h, -1, 0, None, base)
            p_go(u, h, -1, 0, 0, AXES[h][0], 1, base + 2)
            p_got(u, h, 1, 0, None, base + 1)
            p_go(u, h, 1, 0, 1, AXES[h][0], -1, base + 3)

    def first_end(u):
        for h in (0, 1):
            base = 40 * u + 20 * h
            p_got(u, h, 2, 0, 0, base + 2)
            p_got(u, h, 2, 0, 1, base + 3)

    def second_start(u, j):
        for h in (0, 1):
            base = 40 * u + 20 * h + 4 + 4 * j
            p_go(u, h, OFFSET[j], 0, None, AXES[h][1], 1, base)
            p_go(u, h, OFFSET[j], 0, None, AXES[h][1], -1, base + 1)

    def second_pass(u, j):
        for h in (0, 1):
            base = 40 * u + 20 * h + 4 + 4 * j
            p_got(u, h, OFFSET[j], -1, None, base)
            p_go(u, h, OFFSET[j], -1, 0, AXES[h][1], 1, base + 2)
            p_got(u, h, OFFSET[j], 1, None, base + 1)
            p_go(u, h, OFFSET[j], 1, 1, AXES[h][1], -1, base + 3)

    def second_end(u, j):
        for h in (0, 1):
            base = 40 * u + 20 * h + 4 + 4 * j
            p_got(u, h, OFFSET[j], 2, 0, base + 2)
            p_got(u, h, OFFSET[j], 2, 1, base + 3)

    def h_part(step, c, piece=None):
        block = ((x + step) % 4) * 2
        if piece is None:
            return hs.at[pl.ds(block, 2), pl.ds(pl.multiple_of(c * T, T), T), :]
        return hs.at[block + piece, pl.ds(pl.multiple_of(c * T, T), T), :]

    def h_go(step, piece, device, index):
        ref = h_part(step, k, piece)
        go(remote(ref, ref, h_send.at[index], h_recv.at[index], device))

    def h_got(step, c, piece, index):
        got(h_part(step, c, piece), h_recv.at[index])

    def multiply(u, first, count):
        rows = pl.ds(u * U, U)

        def body(n, carry):
            s = ((y + n // 4) % 4) * 4 + (z + n % 4) % 4
            acc[s // 8, rows, :] += jnp.dot(
                ps[s, 0, rows, :], hs[s % 8, pl.ds(0, T), :], preferred_element_type=F32
            ) + jnp.dot(ps[s, 1, rows, :], hs[s % 8, pl.ds(T, T), :], preferred_element_type=F32)
            return carry

        lax.fori_loop(first, first + count, body, 0)

    def f_part(u, step, c, j=None):
        first = ((x + step + plane) % 4) * 4 + 2 * (1 - c)
        return fs.at[u, pl.ds(first, 2)] if j is None else fs.at[u, first + j]

    def f_go(u, step, j, device, index):
        ref = f_part(u, step, k, j)
        go(remote(ref, ref, f_send.at[10 * u + index], f_recv.at[10 * u + index], device))

    def f_got(u, step, c, j, index):
        got(f_part(u, step, c, j), f_recv.at[10 * u + index])

    def scatter(u):
        rows = pl.ds(u * U, U)
        for c in (0, 1):
            first = acc[c, rows, :] * qmask[c, rows, :].astype(F32)
            fb[c, rows, :] = first.astype(BF)
            ft[u, c] = first.T.astype(BF)
            target = dev((y - x) % 4, 2 * k + xh, 2 * xl + c, 1 - zh)
            go(remote(ft.at[u, c], fs.at[u, me], f_send.at[10 * u + c], f_recv.at[10 * u + zl], target))

    def ring_start(u):
        for j in (0, 1):
            f_got(u, 0, k, j, j)
        f_go(u, 0, None, near("x", 1), 2)
        f_go(u, 0, None, near("x", -1), 3)
        f_go(u, 0, None, core, 6)

    def ring_pass(u):
        f_got(u, -1, k, None, 2)
        f_go(u, -1, 0, near("x", 1), 4)
        f_go(u, -1, None, core, 7)
        f_got(u, 1, k, None, 3)
        f_go(u, 1, 1, near("x", -1), 5)
        f_go(u, 1, None, core, 8)

    def ring_end(u):
        f_got(u, 2, k, 0, 4)
        f_got(u, 2, k, 1, 5)
        f_go(u, 2, None, core, 9)

    def multiply_second(u, places):
        def body(n, carry):
            step = sum(jnp.where(n == i, p[0], 0) for i, p in enumerate(places))
            c = sum(jnp.where(n == i, p[1], 0) for i, p in enumerate(places))
            sy = (x + step + plane) % 4
            for j in (0, 1):
                sz = 2 * (1 - c) + j
                for half in (0, 1):
                    sums[half, u] += jnp.dot(
                        ps[half * 8 + (sy % 2) * 4 + sz, sy // 2], fs[u, sy * 4 + sz],
                        preferred_element_type=F32,
                    )
            return carry

        lax.fori_loop(0, len(places), body, 0)

    def columns_of(sy, sz, u):
        return pl.ds(pl.multiple_of(((sy % 2) * 4 + sz) * 2 * T + (sy // 2) * T + u * U, U), U)

    def finish(u):
        columns = pl.ds(u * U, U)
        for c in (0, 1):
            straight = fs[u, (2 * k + xh) * 4 + 2 * xl + c].astype(F32)
            value = straight + fb[c, :, columns].astype(F32) - sums[c, u] * rmask[c, :, columns].astype(F32)
            gs[c, u] = value.astype(BF)

        def rows_for(n):
            ty, tz = (y + n // 4) % 4, (z + n % 4) % 4
            b = (ty % 2) * 4 + tz
            return gs.at[ty // 2, u, pl.ds(pl.multiple_of(b * B, B), B), :], dev(x, ty, tz, k)

        mine = out.at[:, columns_of(y, z, u)]
        local = pltpu.make_async_copy(rows_for(0)[0], mine, o_recv.at[16 * u + me])
        local.start()

        def copy(n):
            rows, device = rows_for(n)
            return remote(rows, mine, o_send.at[16 * u + n], o_recv.at[16 * u + me], device)

        def start(n, carry):
            copy(n).start()
            return carry

        lax.fori_loop(1, 16, start, 0)
        return copy

    q_copies = []
    for side in (0, 1):
        own = mirror & (k == side)
        copy = remote(
            flags.at[2], qv.at[zl], s_send.at[side], s_recv.at[zl],
            dev(2 * yl + zh, 2 * k + xh, 2 * xl + yh, side),
        )
        pl.when(jnp.logical_not(own))(copy.start)
        pl.when(own)(pltpu.make_async_copy(flags.at[2], qv.at[zl], s_recv.at[zl]).start)
        q_copies.append((own, copy))
    go(remote(rv.at[yh], rv.at[yh], s_send.at[2], s_recv.at[2], across))
    home = hs.at[2 * x + yh, pl.ds(pl.multiple_of(k * T, T), T), :]
    go(remote(hm.at[1 - yh], home, h_send.at[0], h_recv.at[0], across))
    h_local = pltpu.make_async_copy(hm.at[yh], home, h_recv.at[1])
    h_local.start()

    first_start(0)
    second_start(0, 0)
    acc[...] = jnp.zeros_like(acc)
    sums[...] = jnp.zeros_like(sums)
    first_pass(0)
    second_start(0, 1)
    second_start(0, 2)

    first_start(1)
    second_start(1, 0)
    h_local.wait()
    got(hs.at[2 * x + 1 - yh, pl.ds(pl.multiple_of(k * T, T), T), :], h_recv.at[0])
    h_go(0, None, near("x", 1), 2)
    h_go(0, None, near("x", -1), 3)
    h_go(0, None, core, 6)
    second_pass(0, 0)
    first_end(0)
    second_start(0, 3)

    for n in (0, 1):
        got(qv.at[n], s_recv.at[n])
    got(rv.at[1 - yh], s_recv.at[2])
    eight = lax.broadcasted_iota(jnp.int32, (8, T), 0) == lax.broadcasted_iota(jnp.int32, (8, T), 1) // B
    narrow = spread(8 * yh)
    for c in (0, 1):
        qexp[...] = lax.dot_general(qv[c], eight.astype(F32), (((0,), (0,)), ((), ())), preferred_element_type=F32)
        q_wide = qexp[pl.ds(pl.multiple_of(k * 8, 8), 8), :]
        r_wide = 2.0 * jnp.dot(rv[c], narrow, preferred_element_type=F32)
        for i in range(8):
            qmask[c, pl.ds(i * B, B), :] = jnp.broadcast_to(q_wide[i : i + 1], (B, T)).astype(BF)
            rmask[c, pl.ds(i * B, B), :] = jnp.broadcast_to(r_wide[i : i + 1], (B, T)).astype(BF)

    second_end(0, 0)
    first_pass(1)
    second_start(1, 1)
    second_start(1, 2)
    second_pass(0, 1)
    second_pass(0, 2)
    h_got(-1, k, None, 2)
    h_go(-1, 0, near("x", 1), 4)
    h_go(-1, None, core, 7)
    h_got(1, k, None, 3)
    h_go(1, 1, near("x", -1), 5)
    h_go(1, None, core, 8)
    second_pass(1, 0)
    second_pass(0, 3)
    first_end(1)
    second_start(1, 3)
    second_end(0, 1)
    second_end(0, 2)
    h_got(2, k, 0, 4)
    h_got(2, k, 1, 5)
    h_go(2, None, core, 9)
    second_end(1, 0)
    second_end(0, 3)
    for n, step in enumerate((0, -1, 1, 2)):
        h_got(step, 1 - k, None, 6 + n)

    multiply(0, 0, 5)
    second_pass(1, 1)
    multiply(0, 5, 5)
    second_pass(1, 2)
    multiply(0, 10, 6)
    scatter(0)
    second_pass(1, 3)
    ring_start(0)
    second_end(1, 1)
    second_end(1, 2)
    ring_pass(0)
    second_end(1, 3)
    multiply(1, 0, 16)
    scatter(1)
    ring_end(0)
    multiply_second(0, [(0, k), (-1, k), (1, k)])
    ring_start(1)
    for n, step in enumerate((0, -1, 1, 2)):
        f_got(0, step, 1 - k, None, 6 + n)
    multiply_second(0, [(2, k), (0, 1 - k), (-1, 1 - k), (1, 1 - k), (2, 1 - k)])
    ring_pass(1)
    o_copy = [finish(0)]
    f_got(1, 0, 1 - k, None, 6)
    multiply_second(1, [(0, k), (-1, k), (1, k), (0, 1 - k)])
    ring_end(1)
    f_got(1, -1, 1 - k, None, 7)
    f_got(1, 1, 1 - k, None, 8)
    multiply_second(1, [(2, k), (-1, 1 - k), (1, 1 - k)])
    f_got(1, 2, 1 - k, None, 9)
    multiply_second(1, [(2, 1 - k)])
    o_copy.append(finish(1))

    for u in (0, 1):
        def take(n, carry, u=u):
            got(out.at[:, columns_of(n // 4, n % 4, u)], o_recv.at[16 * u + n])
            return carry

        lax.fori_loop(0, 16, take, 0)
    for copy in pending:
        copy.wait_send()
    for own, copy in q_copies:
        pl.when(jnp.logical_not(own))(copy.wait_send)
    for copy in o_copy:
        def sent(n, carry, copy=copy):
            copy(n).wait_send()
            return carry

        lax.fori_loop(1, 16, sent, 0)


def per_device(hamiltonian, density, h_flags, p_flags, q_flags, r_flags):
    flags = jnp.stack([h_flags, p_flags, q_flags, r_flags]).astype(F32)
    flags = jnp.pad(flags, ((0, 0), (0, 0), (0, 112)))
    dma = pltpu.SemaphoreType.DMA
    rows = pl.pallas_call(
        kernel,
        out_shape=jax.ShapeDtypeStruct((64, 8192), BF),
        in_specs=[pl.BlockSpec(memory_space=pltpu.VMEM)] * 3,
        out_specs=pl.BlockSpec(memory_space=pl.ANY),
        scratch_shapes=[
            pltpu.VMEM((16, 2, T, T), BF),
            pltpu.VMEM((8, 2 * T, T), BF),
            pltpu.VMEM((2, 16, T, U), BF),
            pltpu.VMEM((2, T, T), BF),
            pltpu.VMEM((2, T, T), F32),
            pltpu.VMEM((2, 2, T, U), F32),
            pltpu.VMEM((2, T, T), BF),
            pltpu.VMEM((2, 2, T, U), BF),
            pltpu.VMEM((2, 2, T, U), BF),
            pltpu.VMEM((2, 8, 128), F32),
            pltpu.VMEM((2, 8, 128), F32),
            pltpu.VMEM((2, T, T), BF),
            pltpu.VMEM((2, T, T), BF),
            pltpu.VMEM((128, T), F32),
            dma((80,)), dma((80,)), dma((10,)), dma((10,)), dma((20,)), dma((20,)),
            dma((3,)), dma((3,)), dma((32,)), dma((32,)),
        ],
        compiler_params=pltpu.CompilerParams(
            collective_id=0, has_side_effects=True, vmem_limit_bytes=60 * 1024 * 1024
        ),
        cost_estimate=pl.CostEstimate(flops=2 * 2 * 512 * 8192 * 1024, bytes_accessed=4 << 20, transcendentals=0),
    )(hamiltonian, density, flags)
    return rows.astype(F32)


def solution(mesh):
    spec = P("row", "col")
    return jax.shard_map(
        per_device,
        mesh=mesh,
        in_specs=(spec,) * 6,
        out_specs=P(("row", "col"), None),
        check_vma=False,
    )
```

time: 548 us -> 191 us (0.35)
  waiting for transfers between devices: 408 us -> 0 us
  Pallas kernels: 0 us -> 185 us
  blocking collectives: 33.2 us -> 0 us
  matrix products: 31.7 us -> 0 us
  local copies, waits for them, and re-layouts: 31.9 us -> 0.61 us
  between operations: 13.3 us -> 0.01 us
  starting transfers between devices: 11.6 us -> 0 us
  other arithmetic: 14.9 us -> 3.42 us
    all_gather x4 -> x0, waiting for transfers between devices: 391 us -> none  [the longest x1 112 us: per_device(): lax.all_gather(first_tile, 'row', axis=0, tiled=True)]
    pallas_call x0 -> x1, Pallas kernels: none -> 185 us  [per_device(): pl.pallas_call(kernel, out_shape=jax.ShapeDtypeStruct((64, 8192), BF), in...]
    all_to_all x1 -> x0, blocking collectives: 33.2 us -> none  [per_device(): lax.all_to_all(second_tile, 'col', split_axis=0, concat_axis=1, tiled=True)]
    dot_general x2 -> x0, matrix products: 31.7 us -> none  [the longest x1 16.1 us: per_device(): jnp.dot(left, lax.all_gather(first_tile, 'row', axis=0, tiled=True), pref...]
    mul x8 -> x0, local copies, waits for them, and re-layouts: 16.8 us -> none  [masked(): shaped * flags.astype(matrix.dtype)[:, None, :, None]]
    all_to_all x2 -> x0, waiting for transfers between devices: 15.5 us -> none  [the longest x1 15.5 us: per_device(): lax.all_to_all(first_send, ('row', 'col'), split_axis=1, concat_axis=0, t...]
    all_to_all x2 -> x0, starting transfers between devices: 11.5 us -> none  [the longest x1 5.95 us: per_device(): lax.all_to_all(first_tile.astype(jnp.float32), 'col', split_axis=0, conca...]
    convert_element_type x4 -> x0, local copies, waits for them, and re-layouts: 7.43 us -> none  [the longest x3 4.61 us: per_device(): first_send = first_line.astype(jnp.bfloat16)]
  transfers between devices with their start and end apart: 6 -> 0, of which waited for: 5 -> 0; matrix products, arithmetic and copies ran while one was open for 10% -> 0% of each run, Pallas kernels for 0% -> 0%
where the time goes in v2:
time: 191 us; the launch traced here: 189 us
  Pallas kernels  185 us (97%)
  other arithmetic  3.42 us (2%)
    pallas_call x1, Pallas kernels, per_device(): pl.pallas_call(kernel, out_shape=jax.ShapeDtypeStruct((64, 8192), BF), in...  185 us

profile of v2, /device:TPU:16, one launch (start us, length us, event | category | flops | bytes accessed | tf_op | source)
XLA Modules:
  0.0 189.4 jit_solution(2470573725532518710)
XLA Ops:
  0.0 0.7 add_convert_fusion
  0.7 0.6 pad.4.flags
  1.4 185.3 %shard_map.64 = bf16[64,8192]{1,0:T(8,128)(2,1)} custom-call(bf16[512,1024]{1,0:T(8,128)(2,1)} %ham.1, bf16[512,1024]{1,0:T(8,128)(2,1)} %den.1, f32[4,8,128]{2,1,0:T(8,128)} %pad.4.flags), custom_call_target="tpu_custom_call" | custom-call | flops 17179869184 | bytes 4194304 | tf_op jit(solution)/shard_map/pallas_call | solution.py:392
  186.7 2.7 %convert_element_type.9 = f32[64,8192]{1,0:T(8,128)} convert(bf16[64,8192]{1,0:T(8,128)(2,1)} %shard_map.64) | non-fusion elementwise | flops 524288 | bytes 3145728 | tf_op jit(solution)/shard_map/convert_element_type | solution.py:420

commit v3 on v2

v3 whole, which is shorter than its diff:
```python
import jax
import jax.numpy as jnp
from jax import lax
from jax.experimental import pallas as pl
from jax.experimental.pallas import tpu as pltpu
from jax.sharding import PartitionSpec as P

MESH = pl.DeviceIdType.MESH
BF = jnp.bfloat16
F32 = jnp.float32
B = 64
T = 512
PARTS = ((0, 256), (256, 128), (384, 128))
STREAMS = (((0, 160), (160, 96)), ((256, 64), (320, 64)), ((384, 64), (448, 64)))
N = len(PARTS)


def dev(x, y, z, k):
    return (x * 4 + (y // 2) * 2 + k, (y % 2) * 4 + z)


def kernel(
    ham, den, flags, out,
    ps, hs, fs, hm, acc, sums, fb, ft, gs, qv, rv, qmask, rmask, qexp,
    p_send, p_recv, h_send, h_recv, f_send, f_recv, s_send, s_recv, o_send, o_recv,
):
    row, col = lax.axis_index("row"), lax.axis_index("col")
    x, yh, k = row // 4, (row // 2) % 2, row % 2
    yl, z = col // 4, col % 4
    y = yh * 2 + yl
    zh, zl = z // 2, z % 2
    xh, xl = x // 2, x % 2
    me = y * 4 + z
    plane = 2 * yl + zh

    def near(axis, step):
        if axis == "x":
            return dev((x + step) % 4, y, z, k)
        if axis == "y":
            return dev(x, (y + step) % 4, z, k)
        return dev(x, y, (z + step) % 4, k)

    core = dev(x, y, z, 1 - k)
    across = near("y", 2)

    def remote(src, dst, send, recv, device):
        return pltpu.make_async_remote_copy(
            src_ref=src, dst_ref=dst, send_sem=send, recv_sem=recv,
            device_id=device, device_id_type=MESH,
        )

    barrier = pltpu.get_barrier_semaphore()

    def greet(device):
        pl.semaphore_signal(barrier, inc=1, device_id=device, device_id_type=MESH)

    def greet_plane(n, carry):
        greet(dev(x, (y + n // 4) % 4, (z + n % 4) % 4, k))
        return carry

    lax.fori_loop(1, 16, greet_plane, 0)
    greet(near("x", 1))
    greet(near("x", -1))
    greet(core)
    for j in (0, 1):
        greet(dev(plane, (x + plane) % 4, 2 * (1 - k) + j, yh))
    mirror = (x == plane) & (y == 2 * k + xh) & (z == 2 * xl + yh)
    for c in (0, 1):
        pl.when(jnp.logical_not(mirror & (zl == c)))(
            lambda c=c: greet(dev(plane, 2 * zl + xh, 2 * xl + c, yh))
        )

    def spread(first):
        blocks = lax.broadcasted_iota(jnp.int32, (128, T), 0)
        places = lax.broadcasted_iota(jnp.int32, (128, T), 1) // B
        return (blocks == places + first).astype(F32)

    wides = [spread(8 * half) for half in (0, 1)]

    def masked(matrix, which, half, i):
        wide = jnp.dot(flags[which], wides[half], preferred_element_type=F32)
        return (matrix[pl.ds(i * B, B), pl.ds(half * T, T)].astype(F32) * wide[i : i + 1]).astype(BF)

    for half in (0, 1):
        for i in range(8):
            ps[me, half, pl.ds(i * B, B), :] = masked(den, 1, half, i)

    pl.semaphore_wait(barrier, 22 - mirror.astype(jnp.int32))

    pending = []

    def go(copy):
        copy.start()
        pending.append(copy)

    def got(dst, recv):
        remote(dst, dst, s_send.at[0], recv, core).wait_recv()

    AXES = (("y", "z"), ("z", "y"))
    OFFSET = (0, -1, 1, 2)

    def p_part(u, h, a, b, part):
        dy, dz = (a, b) if h == 0 else (b, a)
        s = ((y + dy) % 4) * 4 + (z + dz) % 4
        first, size = STREAMS[u][h]
        if part is not None:
            first, size = first + part * (size // 2), size // 2
        return ps.at[s, :, pl.ds(first, size), :]

    def p_go(u, h, a, b, part, axis, step, index):
        ref = p_part(u, h, a, b, part)
        go(remote(ref, ref, p_send.at[index], p_recv.at[index], near(axis, step)))

    def p_got(u, h, a, b, part, index):
        got(p_part(u, h, a, b, part), p_recv.at[index])

    def own(u, h):
        base = 40 * u + 20 * h
        p_go(u, h, 0, 0, None, AXES[h][0], 1, base)
        p_go(u, h, 0, 0, None, AXES[h][0], -1, base + 1)

    def pass_first(u, h, d):
        base, step = 40 * u + 20 * h, 1 - 2 * d
        p_got(u, h, -step, 0, None, base + d)
        p_go(u, h, -step, 0, d, AXES[h][0], step, base + 2 + d)

    def turn(u, h, j):
        base = 40 * u + 20 * h
        if j == 3:
            p_got(u, h, 2, 0, 0, base + 2)
            p_got(u, h, 2, 0, 1, base + 3)
        base += 4 + 4 * j
        p_go(u, h, OFFSET[j], 0, None, AXES[h][1], 1, base)
        p_go(u, h, OFFSET[j], 0, None, AXES[h][1], -1, base + 1)

    def pass_second(u, h, j, d):
        base, step = 40 * u + 20 * h + 4 + 4 * j, 1 - 2 * d
        p_got(u, h, OFFSET[j], -step, None, base + d)
        p_go(u, h, OFFSET[j], -step, d, AXES[h][1], step, base + 2 + d)

    def p_end(u, j):
        for h in (0, 1):
            base = 40 * u + 20 * h + 4 + 4 * j
            p_got(u, h, OFFSET[j], 2, 0, base + 2)
            p_got(u, h, OFFSET[j], 2, 1, base + 3)

    def h_part(step, c, p, part=None):
        first, size = (0, T) if part is None else (part * 256, 256)
        rows = pl.ds(pl.multiple_of(c * T + first, 256), size)
        return hs.at[((x + step) % 4) * 2 + (yh if p == 0 else 1 - yh), rows, :]

    def h_go(step, p, part, device, index):
        ref = h_part(step, k, p, part)
        go(remote(ref, ref, h_send.at[10 * p + index], h_recv.at[10 * p + index], device))

    def h_got(step, c, p, part, index):
        got(h_part(step, c, p, part), h_recv.at[10 * p + index])

    def h_swap():
        for half in (0, 1):
            for i in range(8):
                hm[half, pl.ds(i * B, B), :] = masked(ham, 0, half, i)
        go(remote(hm.at[1 - yh], h_part(0, k, 0), h_send.at[10], h_recv.at[10], across))
        h_local = pltpu.make_async_copy(hm.at[yh], h_part(0, k, 0), h_recv.at[0])
        h_local.start()
        h_local.wait()

    def h_start(p):
        if p == 1:
            h_got(0, k, 1, None, 0)
        h_go(0, p, None, near("x", 1), 2)
        h_go(0, p, None, near("x", -1), 3)
        h_go(0, p, None, core, 6)

    def h_pass(p, d):
        step = 1 - 2 * d
        h_got(-step, k, p, None, 2 + d)
        h_go(-step, p, d, near("x", step), 4 + d)
        h_go(-step, p, None, core, 7 + d)

    def h_end(p):
        h_got(2, k, p, 0, 4)
        h_got(2, k, p, 1, 5)
        h_go(2, p, None, core, 9)

    h_missing = [1]

    def h_ready():
        if h_missing:
            h_missing.clear()
            for p in (0, 1):
                for n, step in enumerate((0, -1, 1, 2)):
                    h_got(step, 1 - k, p, None, 6 + n)

    def multiply_chips(u, chips):
        rows = pl.ds(*PARTS[u])

        def body(i, carry):
            n = sum(jnp.where(i == at, chip, 0) for at, chip in enumerate(chips))
            s = ((y + n // 4) % 4) * 4 + (z + n % 4) % 4
            acc[s // 8, rows, :] += jnp.dot(
                ps[s, 0, rows, :], hs[s % 8, pl.ds(0, T), :], preferred_element_type=F32
            ) + jnp.dot(ps[s, 1, rows, :], hs[s % 8, pl.ds(T, T), :], preferred_element_type=F32)
            return carry

        lax.fori_loop(0, len(chips), body, 0)

    def multiply(u, g):
        h_ready()
        if g == 1:
            p_end(u, 0)
        elif g == 3:
            p_end(u, 1)
            p_end(u, 2)
        elif g == 4:
            p_end(u, 3)
        multiply_chips(u, ((0, 1, 3, 4, 12), (2, 8), (5, 7, 13, 15), (9, 11, 6, 14), (10,))[g])

    def f_part(u, step, c, j=None):
        first = ((x + step + plane) % 4) * 4 + 2 * (1 - c)
        columns = pl.ds(*PARTS[u])
        return fs.at[pl.ds(first, 2), :, columns] if j is None else fs.at[first + j, :, columns]

    def f_go(u, step, j, device, index):
        ref = f_part(u, step, k, j)
        go(remote(ref, ref, f_send.at[10 * u + index], f_recv.at[10 * u + index], device))

    def f_got(u, step, c, j, index):
        got(f_part(u, step, c, j), f_recv.at[10 * u + index])

    def scatter(u):
        rows = pl.ds(*PARTS[u])
        for c in (0, 1):
            first = acc[c, rows, :] * qmask[c, rows, :].astype(F32)
            fb[c, rows, :] = first.astype(BF)
            ft[c, :, rows] = first.T.astype(BF)
            target = dev((y - x) % 4, 2 * k + xh, 2 * xl + c, 1 - zh)
            go(remote(ft.at[c, :, rows], fs.at[me, :, rows], f_send.at[10 * u + c], f_recv.at[10 * u + zl], target))

    def ring_start(u):
        for j in (0, 1):
            f_got(u, 0, k, j, j)
        f_go(u, 0, None, near("x", 1), 2)
        f_go(u, 0, None, near("x", -1), 3)
        f_go(u, 0, None, core, 6)

    def ring_pass(u, d):
        step = 1 - 2 * d
        f_got(u, -step, k, None, 2 + d)
        f_go(u, -step, d, near("x", step), 4 + d)
        f_go(u, -step, None, core, 7 + d)

    def ring_end(u):
        f_got(u, 2, k, 0, 4)
        f_got(u, 2, k, 1, 5)
        f_go(u, 2, None, core, 9)

    def multiply_second(u, r, places):
        rows, columns = pl.ds(256 * r, 256), pl.ds(*PARTS[u])

        def body(n, carry):
            step = sum(jnp.where(n == i, p[0], 0) for i, p in enumerate(places))
            c = sum(jnp.where(n == i, p[1], 0) for i, p in enumerate(places))
            sy = (x + step + plane) % 4
            for j in (0, 1):
                sz = 2 * (1 - c) + j
                for half in (0, 1):
                    sums[half, rows, columns] += jnp.dot(
                        ps[half * 8 + (sy % 2) * 4 + sz, sy // 2, rows, :], fs[sy * 4 + sz, :, columns],
                        preferred_element_type=F32,
                    )
            return carry

        lax.fori_loop(0, len(places), body, 0)

    def second(u, g, r):
        if g == 0:
            if r == 0:
                f_got(u, 0, 1 - k, None, 6)
            multiply_second(u, r, [(0, k), (-1, k), (1, k), (0, 1 - k)])
        else:
            if r == 0:
                f_got(u, -1, 1 - k, None, 7)
                f_got(u, 1, 1 - k, None, 8)
                f_got(u, 2, 1 - k, None, 9)
            multiply_second(u, r, [(2, k), (-1, 1 - k), (1, 1 - k), (2, 1 - k)])

    def columns_of(sy, sz, u):
        first = ((sy % 2) * 4 + sz) * 2 * T + (sy // 2) * T + PARTS[u][0]
        return pl.ds(pl.multiple_of(first, 128), PARTS[u][1])

    o_copy = []

    def finish(u):
        columns = pl.ds(*PARTS[u])
        for c in (0, 1):
            straight = fs[(2 * k + xh) * 4 + 2 * xl + c, :, columns].astype(F32)
            value = straight + fb[c, :, columns].astype(F32)
            gs[c, :, columns] = (value - sums[c, :, columns] * rmask[c, :, columns].astype(F32)).astype(BF)

        def rows_for(n):
            ty, tz = (y + n // 4) % 4, (z + n % 4) % 4
            b = (ty % 2) * 4 + tz
            return gs.at[ty // 2, pl.ds(pl.multiple_of(b * B, B), B), columns], dev(x, ty, tz, k)

        mine = out.at[:, columns_of(y, z, u)]
        local = pltpu.make_async_copy(rows_for(0)[0], mine, o_recv.at[16 * u + me])
        local.start()

        def copy(n):
            rows, device = rows_for(n)
            return remote(rows, mine, o_send.at[16 * u + n], o_recv.at[16 * u + me], device)

        def start(n, carry):
            copy(n).start()
            return carry

        lax.fori_loop(1, 16, start, 0)
        o_copy.append(copy)

    def masks():
        for n in (0, 1):
            got(qv.at[n], s_recv.at[n])
        got(rv.at[1 - yh], s_recv.at[2])
        eight = lax.broadcasted_iota(jnp.int32, (8, T), 0) == lax.broadcasted_iota(jnp.int32, (8, T), 1) // B
        narrow = spread(8 * yh)
        for c in (0, 1):
            qexp[...] = lax.dot_general(qv[c], eight.astype(F32), (((0,), (0,)), ((), ())), preferred_element_type=F32)
            q_wide = qexp[pl.ds(pl.multiple_of(k * 8, 8), 8), :]
            r_wide = 2.0 * jnp.dot(rv[c], narrow, preferred_element_type=F32)
            for i in range(8):
                qmask[c, pl.ds(i * B, B), :] = jnp.broadcast_to(q_wide[i : i + 1], (B, T)).astype(BF)
                rmask[c, pl.ds(i * B, B), :] = jnp.broadcast_to(r_wide[i : i + 1], (B, T)).astype(BF)

    own(0, 0)
    own(0, 1)
    rv[yh] = flags[3]
    q_copies = []
    for side in (0, 1):
        same = mirror & (k == side)
        copy = remote(
            flags.at[2], qv.at[zl], s_send.at[side], s_recv.at[zl],
            dev(2 * yl + zh, 2 * k + xh, 2 * xl + yh, side),
        )
        pl.when(jnp.logical_not(same))(copy.start)
        pl.when(same)(pltpu.make_async_copy(flags.at[2], qv.at[zl], s_recv.at[zl]).start)
        q_copies.append((same, copy))
    go(remote(rv.at[yh], rv.at[yh], s_send.at[2], s_recv.at[2], across))
    acc[...] = jnp.zeros_like(acc)
    sums[...] = jnp.zeros_like(sums)
    h_swap()
    turn(0, 0, 0); turn(0, 1, 0); h_start(0); pass_first(0, 1, 0); turn(0, 1, 1); pass_first(0, 1, 1)
    turn(0, 1, 2); pass_first(0, 0, 0); turn(0, 0, 1); pass_first(0, 0, 1); turn(0, 0, 2); pass_second(0, 0, 0, 0)
    pass_second(0, 0, 0, 1); turn(0, 1, 3); h_pass(0, 0); h_pass(0, 1); h_start(1); pass_second(0, 0, 1, 0)
    pass_second(0, 0, 1, 1); h_end(0); pass_second(0, 1, 0, 0); pass_second(0, 1, 0, 1); pass_second(0, 1, 1, 0)
    pass_second(0, 1, 1, 1); pass_second(0, 0, 2, 0); pass_second(0, 0, 2, 1); pass_second(0, 1, 2, 0)
    pass_second(0, 1, 2, 1); h_pass(1, 0); h_pass(1, 1); turn(0, 0, 3)
    masks()
    pass_second(0, 1, 3, 0); pass_second(0, 1, 3, 1); h_end(1)
    multiply(0, 0)
    own(1, 0); turn(1, 0, 0)
    multiply(0, 1)
    multiply(0, 2)
    pass_second(0, 0, 3, 0); pass_second(0, 0, 3, 1)
    multiply(0, 3)
    pass_second(1, 0, 0, 0); pass_second(1, 0, 0, 1); own(1, 1); turn(1, 1, 0); pass_first(1, 0, 0); turn(1, 0, 1)
    pass_first(1, 0, 1); turn(1, 0, 2)
    multiply(0, 4)
    scatter(0)
    turn(1, 0, 3); pass_second(1, 1, 0, 0); pass_second(1, 1, 0, 1); pass_first(1, 1, 0); turn(1, 1, 1)
    pass_first(1, 1, 1); turn(1, 1, 2)
    multiply(1, 0)
    pass_second(1, 0, 1, 0); pass_second(1, 0, 1, 1); pass_second(1, 0, 2, 0); pass_second(1, 0, 2, 1)
    pass_second(1, 1, 1, 0); pass_second(1, 1, 1, 1); own(2, 0); pass_second(1, 1, 2, 0); pass_second(1, 1, 2, 1)
    turn(2, 0, 0); ring_start(0); pass_second(1, 0, 3, 0); pass_second(1, 0, 3, 1); own(2, 1); turn(2, 1, 0)
    turn(1, 1, 3); pass_first(2, 0, 0); turn(2, 0, 1); pass_first(2, 0, 1); turn(2, 0, 2)
    multiply(1, 1)
    multiply(1, 2)
    pass_second(2, 1, 0, 0); pass_second(2, 1, 0, 1); pass_second(2, 0, 0, 0); pass_second(2, 0, 0, 1)
    pass_second(1, 1, 3, 0); pass_second(1, 1, 3, 1)
    multiply(1, 3)
    turn(2, 0, 3); pass_first(2, 1, 0); turn(2, 1, 1); pass_first(2, 1, 1); turn(2, 1, 2); ring_pass(0, 0)
    ring_pass(0, 1)
    multiply(2, 0)
    multiply(1, 4)
    scatter(1)
    pass_second(2, 0, 1, 0); pass_second(2, 0, 1, 1)
    second(0, 0, 0)
    pass_second(2, 1, 1, 0); pass_second(2, 1, 1, 1); pass_second(2, 0, 2, 0); pass_second(2, 0, 2, 1)
    pass_second(2, 1, 2, 0); pass_second(2, 1, 2, 1); ring_end(0); pass_second(2, 0, 3, 0); pass_second(2, 0, 3, 1)
    turn(2, 1, 3)
    multiply(2, 1)
    multiply(2, 2)
    second(0, 1, 0)
    pass_second(2, 1, 3, 0); pass_second(2, 1, 3, 1); ring_start(1)
    multiply(2, 3)
    multiply(2, 4)
    scatter(2)
    second(0, 0, 1)
    second(0, 1, 1)
    finish(0)
    ring_pass(1, 0); ring_pass(1, 1)
    second(1, 0, 0)
    ring_start(2)
    second(1, 0, 1)
    ring_end(1)
    second(1, 1, 0)
    second(1, 1, 1)
    finish(1)
    ring_pass(2, 0); ring_pass(2, 1)
    second(2, 0, 0)
    second(2, 0, 1)
    ring_end(2)
    second(2, 1, 0)
    second(2, 1, 1)
    finish(2)

    for u in range(N):
        def take(n, carry, u=u):
            got(out.at[:, columns_of(n // 4, n % 4, u)], o_recv.at[16 * u + n])
            return carry

        lax.fori_loop(0, 16, take, 0)
    for copy in pending:
        copy.wait_send()
    for same, copy in q_copies:
        pl.when(jnp.logical_not(same))(copy.wait_send)
    for copy in o_copy:
        def sent(n, carry, copy=copy):
            copy(n).wait_send()
            return carry

        lax.fori_loop(1, 16, sent, 0)


def per_device(hamiltonian, density, h_flags, p_flags, q_flags, r_flags):
    flags = jnp.stack([h_flags, p_flags, q_flags, r_flags]).astype(F32)
    flags = jnp.pad(flags, ((0, 0), (0, 0), (0, 112)))
    dma = pltpu.SemaphoreType.DMA
    rows = pl.pallas_call(
        kernel,
        out_shape=jax.ShapeDtypeStruct((64, 8192), BF),
        in_specs=[pl.BlockSpec(memory_space=pltpu.VMEM)] * 3,
        out_specs=pl.BlockSpec(memory_space=pl.ANY),
        scratch_shapes=[
            pltpu.VMEM((16, 2, T, T), BF),
            pltpu.VMEM((8, 2 * T, T), BF),
            pltpu.VMEM((16, T, T), BF),
            pltpu.VMEM((2, T, T), BF),
            pltpu.VMEM((2, T, T), F32),
            pltpu.VMEM((2, T, T), F32),
            pltpu.VMEM((2, T, T), BF),
            pltpu.VMEM((2, T, T), BF),
            pltpu.VMEM((2, T, T), BF),
            pltpu.VMEM((2, 8, 128), F32),
            pltpu.VMEM((2, 8, 128), F32),
            pltpu.VMEM((2, T, T), BF),
            pltpu.VMEM((2, T, T), BF),
            pltpu.VMEM((128, T), F32),
            dma((40 * N,)), dma((40 * N,)), dma((20,)), dma((20,)), dma((10 * N,)), dma((10 * N,)),
            dma((3,)), dma((3,)), dma((16 * N,)), dma((16 * N,)),
        ],
        compiler_params=pltpu.CompilerParams(
            collective_id=0, has_side_effects=True, vmem_limit_bytes=60 * 1024 * 1024
        ),
        cost_estimate=pl.CostEstimate(flops=2 * 2 * 512 * 8192 * 1024, bytes_accessed=4 << 20, transcendentals=0),
    )(hamiltonian, density, flags)
    return rows.astype(F32)


def solution(mesh):
    spec = P("row", "col")
    return jax.shard_map(
        per_device,
        mesh=mesh,
        in_specs=(spec,) * 6,
        out_specs=P(("row", "col"), None),
        check_vma=False,
    )
```

time: 191 us -> 169 us (0.88)
  Pallas kernels: 185 us -> 163 us
    pallas_call x1, Pallas kernels: 185 us -> 163 us  [per_device(): pl.pallas_call(kernel, out_shape=jax.ShapeDtypeStruct((64, 8192), BF), in...]
where the time goes in v3:
time: 169 us; the launch traced here: 168 us
  Pallas kernels  163 us (96%)
  other arithmetic  3.42 us (2%)
    pallas_call x1, Pallas kernels, per_device(): pl.pallas_call(kernel, out_shape=jax.ShapeDtypeStruct((64, 8192), BF), in...  163 us

profile of v3, /device:TPU:16, one launch (start us, length us, event | category | flops | bytes accessed | tf_op | source)
XLA Modules:
  0.0 167.5 jit_solution(14114802281974212515)
XLA Ops:
  0.0 0.7 add_convert_fusion
  0.7 0.6 pad.4.flags
  1.4 163.5 %shard_map.64 = bf16[64,8192]{1,0:T(8,128)(2,1)} custom-call(bf16[512,1024]{1,0:T(8,128)(2,1)} %ham.1, bf16[512,1024]{1,0:T(8,128)(2,1)} %den.1, f32[4,8,128]{2,1,0:T(8,128)} %pad.4.flags), custom_call_target="tpu_custom_call" | custom-call | flops 17179869184 | bytes 4194304 | tf_op jit(solution)/shard_map/pallas_call | solution.py:440
  164.9 2.7 %convert_element_type.9 = f32[64,8192]{1,0:T(8,128)} convert(bf16[64,8192]{1,0:T(8,128)(2,1)} %shard_map.64) | non-fusion elementwise | flops 524288 | bytes 3145728 | tf_op jit(solution)/shard_map/convert_element_type | solution.py:468

commit v4 on v3

--- a/solution.py
+++ b/solution.py
@@ -63,7 +63,7 @@
     greet(near("x", -1))
     greet(core)
     for j in (0, 1):
-        greet(dev(plane, (x + plane) % 4, 2 * (1 - k) + j, yh))
+        greet(dev(plane, (x + plane + 2 * zl) % 4, 2 * ((1 - k + zl) % 2) + j, yh))
     mirror = (x == plane) & (y == 2 * k + xh) & (z == 2 * xl + yh)
     for c in (0, 1):
         pl.when(jnp.logical_not(mirror & (zl == c)))(
@@ -192,15 +192,22 @@
                 for n, step in enumerate((0, -1, 1, 2)):
                     h_got(step, 1 - k, p, None, 6 + n)
 
+    def pick(i, values):
+        return sum(jnp.where(i == at, value, 0) for at, value in enumerate(values))
+
     def multiply_chips(u, chips):
-        rows = pl.ds(*PARTS[u])
+        first, size = PARTS[u]
+        rows = pl.ds(first, size)
 
         def body(i, carry):
-            n = sum(jnp.where(i == at, chip, 0) for at, chip in enumerate(chips))
-            s = ((y + n // 4) % 4) * 4 + (z + n % 4) % 4
-            acc[s // 8, rows, :] += jnp.dot(
-                ps[s, 0, rows, :], hs[s % 8, pl.ds(0, T), :], preferred_element_type=F32
-            ) + jnp.dot(ps[s, 1, rows, :], hs[s % 8, pl.ds(T, T), :], preferred_element_type=F32)
+            n = pick(i, chips)
+            s = ((y + n // 4) % 2) * 4 + (z + n % 4) % 4
+            left = jnp.concatenate(
+                [jnp.concatenate([ps[s + 8 * c, half, rows, :] for half in (0, 1)], axis=1) for c in (0, 1)], axis=0
+            )
+            found = jnp.dot(left, hs[s], preferred_element_type=F32)
+            for c in (0, 1):
+                acc[c, rows, :] += found[c * size : (c + 1) * size]
             return carry
 
         lax.fori_loop(0, len(chips), body, 0)
@@ -214,10 +221,10 @@
             p_end(u, 2)
         elif g == 4:
             p_end(u, 3)
-        multiply_chips(u, ((0, 1, 3, 4, 12), (2, 8), (5, 7, 13, 15), (9, 11, 6, 14), (10,))[g])
+        multiply_chips(u, ((4,), (0,), (5, 7), (1, 3, 6), (2,))[g])
 
     def f_part(u, step, c, j=None):
-        first = ((x + step + plane) % 4) * 4 + 2 * (1 - c)
+        first = ((x + step + plane + 2 * zl) % 4) * 4 + 2 * ((1 - c + zl) % 2)
         columns = pl.ds(*PARTS[u])
         return fs.at[pl.ds(first, 2), :, columns] if j is None else fs.at[first + j, :, columns]
 
@@ -234,7 +241,7 @@
             first = acc[c, rows, :] * qmask[c, rows, :].astype(F32)
             fb[c, rows, :] = first.astype(BF)
             ft[c, :, rows] = first.T.astype(BF)
-            target = dev((y - x) % 4, 2 * k + xh, 2 * xl + c, 1 - zh)
+            target = dev((y - x + 2 * c) % 4, 2 * k + xh, 2 * xl + c, (1 - zh + c) % 2)
             go(remote(ft.at[c, :, rows], fs.at[me, :, rows], f_send.at[10 * u + c], f_recv.at[10 * u + zl], target))
 
     def ring_start(u):
@@ -255,44 +262,56 @@
         f_got(u, 2, k, 1, 5)
         f_go(u, 2, None, core, 9)
 
-    def multiply_second(u, r, places):
-        rows, columns = pl.ds(256 * r, 256), pl.ds(*PARTS[u])
+    def multiply_second(v, which, places):
+        rows, columns, size = pl.ds(*which), pl.ds(256 * v, 256), which[1]
 
         def body(n, carry):
-            step = sum(jnp.where(n == i, p[0], 0) for i, p in enumerate(places))
-            c = sum(jnp.where(n == i, p[1], 0) for i, p in enumerate(places))
-            sy = (x + step + plane) % 4
+            step = pick(n, [p[0] for p in places])
+            c = pick(n, [p[1] for p in places])
+            sy = (x + step + plane + 2 * zl) % 4
+            sz = 2 * ((1 - c + zl) % 2)
+            found = 0
             for j in (0, 1):
-                sz = 2 * (1 - c) + j
-                for half in (0, 1):
-                    sums[half, rows, columns] += jnp.dot(
-                        ps[half * 8 + (sy % 2) * 4 + sz, sy // 2, rows, :], fs[sy * 4 + sz, :, columns],
-                        preferred_element_type=F32,
-                    )
+                s = (sy % 2) * 4 + sz + j
+                left = jnp.concatenate([ps[s + 8 * half, sy // 2, rows, :] for half in (0, 1)], axis=0)
+                found += jnp.dot(left, fs[sy * 4 + sz + j, :, columns], preferred_element_type=F32)
+            for half in (0, 1):
+                sums[half, rows, columns] += found[half * size : (half + 1) * size]
             return carry
 
         lax.fori_loop(0, len(places), body, 0)
 
-    def second(u, g, r):
-        if g == 0:
-            if r == 0:
+    def second(v, g):
+        if v == 0 and g < 2:
+            if g == 0:
+                f_got(0, 0, 1 - k, None, 6)
+                multiply_second(0, (0, 256), [(0, k), (-1, k), (1, k), (0, 1 - k)])
+            else:
+                f_got(0, -1, 1 - k, None, 7)
+                f_got(0, 1, 1 - k, None, 8)
+                f_got(0, 2, 1 - k, None, 9)
+                multiply_second(0, (0, 256), [(2, k), (-1, 1 - k), (1, 1 - k), (2, 1 - k)])
+        elif v == 0:
+            multiply_second(0, (256, 256), [(s, c) for s in OFFSET for c in (k, 1 - k)])
+        elif g == 0:
+            for u in range(1, N):
                 f_got(u, 0, 1 - k, None, 6)
-            multiply_second(u, r, [(0, k), (-1, k), (1, k), (0, 1 - k)])
+            multiply_second(1, (0, T), [(0, k), (-1, k), (1, k), (0, 1 - k)])
         else:
-            if r == 0:
+            for u in range(1, N):
                 f_got(u, -1, 1 - k, None, 7)
                 f_got(u, 1, 1 - k, None, 8)
                 f_got(u, 2, 1 - k, None, 9)
-            multiply_second(u, r, [(2, k), (-1, 1 - k), (1, 1 - k), (2, 1 - k)])
-
-    def columns_of(sy, sz, u):
-        first = ((sy % 2) * 4 + sz) * 2 * T + (sy // 2) * T + PARTS[u][0]
-        return pl.ds(pl.multiple_of(first, 128), PARTS[u][1])
+            multiply_second(1, (0, T), [(2, k), (-1, 1 - k), (1, 1 - k), (2, 1 - k)])
+
+    def columns_of(sy, sz, v):
+        first = ((sy % 2) * 4 + sz) * 2 * T + (sy // 2) * T + 256 * v
+        return pl.ds(pl.multiple_of(first, 256), 256)
 
     o_copy = []
 
     def finish(u):
-        columns = pl.ds(*PARTS[u])
+        columns = pl.ds(256 * u, 256)
         for c in (0, 1):
             straight = fs[(2 * k + xh) * 4 + 2 * xl + c, :, columns].astype(F32)
             value = straight + fb[c, :, columns].astype(F32)
@@ -372,50 +391,40 @@
     multiply(1, 0)
     pass_second(1, 0, 1, 0); pass_second(1, 0, 1, 1); pass_second(1, 0, 2, 0); pass_second(1, 0, 2, 1)
     pass_second(1, 1, 1, 0); pass_second(1, 1, 1, 1); own(2, 0); pass_second(1, 1, 2, 0); pass_second(1, 1, 2, 1)
-    turn(2, 0, 0); ring_start(0); pass_second(1, 0, 3, 0); pass_second(1, 0, 3, 1); own(2, 1); turn(2, 1, 0)
-    turn(1, 1, 3); pass_first(2, 0, 0); turn(2, 0, 1); pass_first(2, 0, 1); turn(2, 0, 2)
+    turn(2, 0, 0); ring_start(0); pass_second(1, 0, 3, 0); pass_second(1, 0, 3, 1); turn(1, 1, 3)
     multiply(1, 1)
+    pass_first(2, 0, 0); turn(2, 0, 1); pass_first(2, 0, 1); turn(2, 0, 2)
     multiply(1, 2)
-    pass_second(2, 1, 0, 0); pass_second(2, 1, 0, 1); pass_second(2, 0, 0, 0); pass_second(2, 0, 0, 1)
-    pass_second(1, 1, 3, 0); pass_second(1, 1, 3, 1)
+    own(2, 1); turn(2, 1, 0); pass_second(1, 1, 3, 0); pass_second(1, 1, 3, 1)
     multiply(1, 3)
-    turn(2, 0, 3); pass_first(2, 1, 0); turn(2, 1, 1); pass_first(2, 1, 1); turn(2, 1, 2); ring_pass(0, 0)
-    ring_pass(0, 1)
-    multiply(2, 0)
+    turn(2, 0, 3); pass_second(2, 0, 0, 0); pass_second(2, 0, 0, 1); pass_second(2, 1, 0, 0)
+    pass_second(2, 1, 0, 1); pass_second(2, 0, 1, 0); pass_second(2, 0, 1, 1); ring_pass(0, 0); ring_pass(0, 1)
     multiply(1, 4)
     scatter(1)
-    pass_second(2, 0, 1, 0); pass_second(2, 0, 1, 1)
-    second(0, 0, 0)
-    pass_second(2, 1, 1, 0); pass_second(2, 1, 1, 1); pass_second(2, 0, 2, 0); pass_second(2, 0, 2, 1)
-    pass_second(2, 1, 2, 0); pass_second(2, 1, 2, 1); ring_end(0); pass_second(2, 0, 3, 0); pass_second(2, 0, 3, 1)
-    turn(2, 1, 3)
+    pass_second(2, 0, 2, 0); pass_second(2, 0, 2, 1)
+    second(0, 0)
+    pass_first(2, 1, 0); turn(2, 1, 1); pass_first(2, 1, 1); turn(2, 1, 2)
+    multiply(2, 0)
+    ring_end(0); pass_second(2, 0, 3, 0); pass_second(2, 0, 3, 1); pass_second(2, 1, 1, 0); pass_second(2, 1, 1, 1)
+    second(0, 1)
+    pass_second(2, 1, 2, 0); pass_second(2, 1, 2, 1); ring_start(1); turn(2, 1, 3)
     multiply(2, 1)
     multiply(2, 2)
-    second(0, 1, 0)
-    pass_second(2, 1, 3, 0); pass_second(2, 1, 3, 1); ring_start(1)
+    pass_second(2, 1, 3, 0); pass_second(2, 1, 3, 1)
     multiply(2, 3)
+    ring_pass(1, 0); ring_pass(1, 1)
     multiply(2, 4)
     scatter(2)
-    second(0, 0, 1)
-    second(0, 1, 1)
+    second(0, 2)
+    ring_end(1)
     finish(0)
-    ring_pass(1, 0); ring_pass(1, 1)
-    second(1, 0, 0)
-    ring_start(2)
-    second(1, 0, 1)
-    ring_end(1)
-    second(1, 1, 0)
-    second(1, 1, 1)
+    ring_start(2); ring_pass(2, 0); ring_pass(2, 1)
+    second(1, 0)
+    ring_end(2)
+    second(1, 1)
     finish(1)
-    ring_pass(2, 0); ring_pass(2, 1)
-    second(2, 0, 0)
-    second(2, 0, 1)
-    ring_end(2)
-    second(2, 1, 0)
-    second(2, 1, 1)
-    finish(2)
-
-    for u in range(N):
+
+    for u in (0, 1):
         def take(n, carry, u=u):
             got(out.at[:, columns_of(n // 4, n % 4, u)], o_recv.at[16 * u + n])
             return carry
@@ -458,7 +467,7 @@
             pltpu.VMEM((2, T, T), BF),
             pltpu.VMEM((128, T), F32),
             dma((40 * N,)), dma((40 * N,)), dma((20,)), dma((20,)), dma((10 * N,)), dma((10 * N,)),
-            dma((3,)), dma((3,)), dma((16 * N,)), dma((16 * N,)),
+            dma((3,)), dma((3,)), dma((32,)), dma((32,)),
         ],
         compiler_params=pltpu.CompilerParams(
             collective_id=0, has_side_effects=True, vmem_limit_bytes=60 * 1024 * 1024

time: 169 us -> 168 us (level)
    pallas_call x1, Pallas kernels: 163 us -> 162 us  [per_device(): pl.pallas_call(kernel, out_shape=jax.ShapeDtypeStruct((64, 8192), BF), in...]
where the time goes in v4:
time: 168 us; the launch traced here: 166 us
  Pallas kernels  162 us (96%)
  other arithmetic  3.42 us (2%)
    pallas_call x1, Pallas kernels, per_device(): pl.pallas_call(kernel, out_shape=jax.ShapeDtypeStruct((64, 8192), BF), in...  162 us

profile of v4, /device:TPU:16, one launch (start us, length us, event | category | flops | bytes accessed | tf_op | source)
XLA Modules:
  0.0 165.7 jit_solution(7988863352802425176)
XLA Ops:
  0.0 0.7 add_convert_fusion
  0.7 0.6 pad.4.flags
  1.4 161.7 %shard_map.64 = bf16[64,8192]{1,0:T(8,128)(2,1)} custom-call(bf16[512,1024]{1,0:T(8,128)(2,1)} %ham.1, bf16[512,1024]{1,0:T(8,128)(2,1)} %den.1, f32[4,8,128]{2,1,0:T(8,128)} %pad.4.flags), custom_call_target="tpu_custom_call" | custom-call | flops 17179869184 | bytes 4194304 | tf_op jit(solution)/shard_map/pallas_call | solution.py:449
  163.1 2.7 %convert_element_type.9 = f32[64,8192]{1,0:T(8,128)} convert(bf16[64,8192]{1,0:T(8,128)(2,1)} %shard_map.64) | non-fusion elementwise | flops 524288 | bytes 3145728 | tf_op jit(solution)/shard_map/convert_element_type | solution.py:477

commit v5 on v4

--- a/solution.py
+++ b/solution.py
@@ -11,7 +11,7 @@
 B = 64
 T = 512
 PARTS = ((0, 256), (256, 128), (384, 128))
-STREAMS = (((0, 160), (160, 96)), ((256, 64), (320, 64)), ((384, 64), (448, 64)))
+STREAMS = (((0, 144), (144, 112)), ((256, 64), (320, 64)), ((384, 64), (448, 64)))
 N = len(PARTS)
 
 
@@ -104,7 +104,8 @@
         s = ((y + dy) % 4) * 4 + (z + dz) % 4
         first, size = STREAMS[u][h]
         if part is not None:
-            first, size = first + part * (size // 2), size // 2
+            cut = (size // 2 + 15) // 16 * 16
+            first, size = (first, cut) if part == 0 else (first + cut, size - cut)
         return ps.at[s, :, pl.ds(first, size), :]
 
     def p_go(u, h, a, b, part, axis, step, index):
@@ -351,8 +352,7 @@
                 qmask[c, pl.ds(i * B, B), :] = jnp.broadcast_to(q_wide[i : i + 1], (B, T)).astype(BF)
                 rmask[c, pl.ds(i * B, B), :] = jnp.broadcast_to(r_wide[i : i + 1], (B, T)).astype(BF)
 
-    own(0, 0)
-    own(0, 1)
+    own(0, 0); own(0, 1)
     rv[yh] = flags[3]
     q_copies = []
     for side in (0, 1):
@@ -368,57 +368,54 @@
     acc[...] = jnp.zeros_like(acc)
     sums[...] = jnp.zeros_like(sums)
     h_swap()
-    turn(0, 0, 0); turn(0, 1, 0); h_start(0); pass_first(0, 1, 0); turn(0, 1, 1); pass_first(0, 1, 1)
+    h_start(0); turn(0, 1, 0); turn(0, 0, 0); pass_first(0, 1, 0); turn(0, 1, 1); pass_first(0, 1, 1)
     turn(0, 1, 2); pass_first(0, 0, 0); turn(0, 0, 1); pass_first(0, 0, 1); turn(0, 0, 2); pass_second(0, 0, 0, 0)
-    pass_second(0, 0, 0, 1); turn(0, 1, 3); h_pass(0, 0); h_pass(0, 1); h_start(1); pass_second(0, 0, 1, 0)
-    pass_second(0, 0, 1, 1); h_end(0); pass_second(0, 1, 0, 0); pass_second(0, 1, 0, 1); pass_second(0, 1, 1, 0)
-    pass_second(0, 1, 1, 1); pass_second(0, 0, 2, 0); pass_second(0, 0, 2, 1); pass_second(0, 1, 2, 0)
-    pass_second(0, 1, 2, 1); h_pass(1, 0); h_pass(1, 1); turn(0, 0, 3)
+    pass_second(0, 0, 0, 1); h_pass(0, 0); h_pass(0, 1); turn(0, 1, 3); h_start(1); pass_second(0, 0, 1, 0)
+    pass_second(0, 0, 1, 1); h_end(0); pass_second(0, 1, 0, 0); pass_second(0, 1, 0, 1); pass_second(0, 0, 2, 0)
+    pass_second(0, 0, 2, 1); pass_second(0, 1, 1, 0); pass_second(0, 1, 1, 1); pass_second(0, 1, 2, 0)
+    pass_second(0, 1, 2, 1); h_pass(1, 0); own(1, 0); turn(1, 0, 0); h_pass(1, 1); turn(0, 0, 3)
     masks()
-    pass_second(0, 1, 3, 0); pass_second(0, 1, 3, 1); h_end(1)
+    pass_second(1, 0, 0, 0); pass_second(1, 0, 0, 1); pass_second(0, 1, 3, 0); pass_second(0, 1, 3, 1); h_end(1)
+    own(1, 1); turn(1, 1, 0); pass_second(0, 0, 3, 0); pass_second(0, 0, 3, 1)
     multiply(0, 0)
-    own(1, 0); turn(1, 0, 0)
     multiply(0, 1)
     multiply(0, 2)
-    pass_second(0, 0, 3, 0); pass_second(0, 0, 3, 1)
+    pass_first(1, 1, 0); turn(1, 1, 1); pass_first(1, 1, 1); turn(1, 1, 2); pass_first(1, 0, 0); turn(1, 0, 1)
+    pass_first(1, 0, 1); turn(1, 0, 2)
     multiply(0, 3)
-    pass_second(1, 0, 0, 0); pass_second(1, 0, 0, 1); own(1, 1); turn(1, 1, 0); pass_first(1, 0, 0); turn(1, 0, 1)
-    pass_first(1, 0, 1); turn(1, 0, 2)
     multiply(0, 4)
     scatter(0)
-    turn(1, 0, 3); pass_second(1, 1, 0, 0); pass_second(1, 1, 0, 1); pass_first(1, 1, 0); turn(1, 1, 1)
-    pass_first(1, 1, 1); turn(1, 1, 2)
+    turn(1, 1, 3); pass_second(1, 1, 0, 0); pass_second(1, 1, 0, 1)
     multiply(1, 0)
-    pass_second(1, 0, 1, 0); pass_second(1, 0, 1, 1); pass_second(1, 0, 2, 0); pass_second(1, 0, 2, 1)
-    pass_second(1, 1, 1, 0); pass_second(1, 1, 1, 1); own(2, 0); pass_second(1, 1, 2, 0); pass_second(1, 1, 2, 1)
-    turn(2, 0, 0); ring_start(0); pass_second(1, 0, 3, 0); pass_second(1, 0, 3, 1); turn(1, 1, 3)
+    pass_second(1, 0, 1, 0); pass_second(1, 0, 1, 1); pass_second(1, 1, 1, 0); pass_second(1, 1, 1, 1)
+    pass_second(1, 0, 2, 0); pass_second(1, 0, 2, 1); pass_second(1, 1, 2, 0); pass_second(1, 1, 2, 1)
+    turn(1, 0, 3); own(2, 0); turn(2, 0, 0); ring_start(0); own(2, 1); pass_second(1, 0, 3, 0)
+    pass_second(1, 1, 3, 0); pass_second(1, 1, 3, 1); pass_second(1, 0, 3, 1); turn(2, 1, 0)
     multiply(1, 1)
-    pass_first(2, 0, 0); turn(2, 0, 1); pass_first(2, 0, 1); turn(2, 0, 2)
     multiply(1, 2)
-    own(2, 1); turn(2, 1, 0); pass_second(1, 1, 3, 0); pass_second(1, 1, 3, 1)
+    pass_second(2, 0, 0, 0); pass_second(2, 0, 0, 1)
     multiply(1, 3)
-    turn(2, 0, 3); pass_second(2, 0, 0, 0); pass_second(2, 0, 0, 1); pass_second(2, 1, 0, 0)
-    pass_second(2, 1, 0, 1); pass_second(2, 0, 1, 0); pass_second(2, 0, 1, 1); ring_pass(0, 0); ring_pass(0, 1)
+    pass_first(2, 1, 0); turn(2, 1, 1); pass_first(2, 1, 1); turn(2, 1, 2); pass_first(2, 0, 0); turn(2, 0, 1)
+    pass_first(2, 0, 1); turn(2, 0, 2)
     multiply(1, 4)
     scatter(1)
-    pass_second(2, 0, 2, 0); pass_second(2, 0, 2, 1)
+    turn(2, 1, 3); pass_second(2, 1, 0, 0); pass_second(2, 1, 0, 1)
+    multiply(2, 0)
+    pass_second(2, 0, 1, 0); ring_pass(0, 0); ring_pass(0, 1); pass_second(2, 0, 1, 1)
     second(0, 0)
-    pass_first(2, 1, 0); turn(2, 1, 1); pass_first(2, 1, 1); turn(2, 1, 2)
-    multiply(2, 0)
-    ring_end(0); pass_second(2, 0, 3, 0); pass_second(2, 0, 3, 1); pass_second(2, 1, 1, 0); pass_second(2, 1, 1, 1)
-    second(0, 1)
-    pass_second(2, 1, 2, 0); pass_second(2, 1, 2, 1); ring_start(1); turn(2, 1, 3)
+    pass_second(2, 1, 1, 0); pass_second(2, 1, 1, 1); pass_second(2, 0, 2, 0); pass_second(2, 0, 2, 1)
+    pass_second(2, 1, 2, 0); pass_second(2, 1, 2, 1); turn(2, 0, 3); ring_end(0); ring_start(1)
+    pass_second(2, 1, 3, 0); pass_second(2, 1, 3, 1); pass_second(2, 0, 3, 0); pass_second(2, 0, 3, 1)
     multiply(2, 1)
     multiply(2, 2)
-    pass_second(2, 1, 3, 0); pass_second(2, 1, 3, 1)
+    second(0, 1)
     multiply(2, 3)
-    ring_pass(1, 0); ring_pass(1, 1)
     multiply(2, 4)
     scatter(2)
     second(0, 2)
-    ring_end(1)
+    ring_pass(1, 0); ring_pass(1, 1)
     finish(0)
-    ring_start(2); ring_pass(2, 0); ring_pass(2, 1)
+    ring_start(2); ring_end(1); ring_pass(2, 0); ring_pass(2, 1)
     second(1, 0)
     ring_end(2)
     second(1, 1)

time: 168 us -> 160 us (0.952); the launches traced: 166 us -> 160 us
  Pallas kernels: 162 us -> 156 us
    pallas_call x1, Pallas kernels: 162 us -> 156 us  [per_device(): pl.pallas_call(kernel, out_shape=jax.ShapeDtypeStruct((64, 8192), BF), in...]
where the time goes in v5:
time: 160 us
  Pallas kernels  156 us (98%)
  other arithmetic  3.42 us (2%)
    pallas_call x1, Pallas kernels, per_device(): pl.pallas_call(kernel, out_shape=jax.ShapeDtypeStruct((64, 8192), BF), in...  156 us

profile of v5, /device:TPU:16, one launch (start us, length us, event | category | flops | bytes accessed | tf_op | source)
XLA Modules:
  0.0 160.0 jit_solution(12772537526948449556)
XLA Ops:
  0.0 0.7 add_convert_fusion
  0.7 0.6 pad.4.flags
  1.4 155.9 %shard_map.64 = bf16[64,8192]{1,0:T(8,128)(2,1)} custom-call(bf16[512,1024]{1,0:T(8,128)(2,1)} %ham.1, bf16[512,1024]{1,0:T(8,128)(2,1)} %den.1, f32[4,8,128]{2,1,0:T(8,128)} %pad.4.flags), custom_call_target="tpu_custom_call" | custom-call | flops 17179869184 | bytes 4194304 | tf_op jit(solution)/shard_map/pallas_call | solution.py:446
  157.3 2.7 %convert_element_type.9 = f32[64,8192]{1,0:T(8,128)} convert(bf16[64,8192]{1,0:T(8,128)(2,1)} %shard_map.64) | non-fusion elementwise | flops 524288 | bytes 3145728 | tf_op jit(solution)/shard_map/convert_element_type | solution.py:474

commit v6 on v5

--- a/solution.py
+++ b/solution.py
@@ -20,8 +20,8 @@
 
 
 def kernel(
-    ham, den, flags, out,
-    ps, hs, fs, hm, acc, sums, fb, ft, gs, qv, rv, qmask, rmask, qexp,
+    ham, den, h_flags, p_flags, q_flags, r_flags, out,
+    flags, ps, hs, fs, hm, acc, sums, fb, ft, gs, qv, rv, qmask, rmask, qexp,
     p_send, p_recv, h_send, h_recv, f_send, f_recv, s_send, s_recv, o_send, o_recv,
 ):
     row, col = lax.axis_index("row"), lax.axis_index("col")
@@ -75,15 +75,22 @@
         places = lax.broadcasted_iota(jnp.int32, (128, T), 1) // B
         return (blocks == places + first).astype(F32)
 
+    flags[...] = jnp.zeros_like(flags)
+    for n, given in enumerate((h_flags, p_flags, q_flags, r_flags)):
+        flags[n, :, pl.ds(0, 16)] = given[...].astype(F32)
     wides = [spread(8 * half) for half in (0, 1)]
 
-    def masked(matrix, which, half, i):
-        wide = jnp.dot(flags[which], wides[half], preferred_element_type=F32)
+    h_wides, p_wides = [
+        [jnp.dot(flags[which], wide, preferred_element_type=F32) for wide in wides] for which in (0, 1)
+    ]
+
+    def masked(matrix, blocks, half, i):
+        wide = blocks[half]
         return (matrix[pl.ds(i * B, B), pl.ds(half * T, T)].astype(F32) * wide[i : i + 1]).astype(BF)
 
     for half in (0, 1):
         for i in range(8):
-            ps[me, half, pl.ds(i * B, B), :] = masked(den, 1, half, i)
+            ps[me, half, pl.ds(i * B, B), :] = masked(den, p_wides, half, i)
 
     pl.semaphore_wait(barrier, 22 - mirror.astype(jnp.int32))
 
@@ -160,7 +167,7 @@
     def h_swap():
         for half in (0, 1):
             for i in range(8):
-                hm[half, pl.ds(i * B, B), :] = masked(ham, 0, half, i)
+                hm[half, pl.ds(i * B, B), :] = masked(ham, h_wides, half, i)
         go(remote(hm.at[1 - yh], h_part(0, k, 0), h_send.at[10], h_recv.at[10], across))
         h_local = pltpu.make_async_copy(hm.at[yh], h_part(0, k, 0), h_recv.at[0])
         h_local.start()
@@ -440,15 +447,14 @@
 
 
 def per_device(hamiltonian, density, h_flags, p_flags, q_flags, r_flags):
-    flags = jnp.stack([h_flags, p_flags, q_flags, r_flags]).astype(F32)
-    flags = jnp.pad(flags, ((0, 0), (0, 0), (0, 112)))
     dma = pltpu.SemaphoreType.DMA
     rows = pl.pallas_call(
         kernel,
         out_shape=jax.ShapeDtypeStruct((64, 8192), BF),
-        in_specs=[pl.BlockSpec(memory_space=pltpu.VMEM)] * 3,
+        in_specs=[pl.BlockSpec(memory_space=pltpu.VMEM)] * 6,
         out_specs=pl.BlockSpec(memory_space=pl.ANY),
         scratch_shapes=[
+            pltpu.VMEM((4, 8, 128), F32),
             pltpu.VMEM((16, 2, T, T), BF),
             pltpu.VMEM((8, 2 * T, T), BF),
             pltpu.VMEM((16, T, T), BF),
@@ -470,7 +476,7 @@
             collective_id=0, has_side_effects=True, vmem_limit_bytes=60 * 1024 * 1024
         ),
         cost_estimate=pl.CostEstimate(flops=2 * 2 * 512 * 8192 * 1024, bytes_accessed=4 << 20, transcendentals=0),
-    )(hamiltonian, density, flags)
+    )(hamiltonian, density, h_flags, p_flags, q_flags, r_flags)
     return rows.astype(F32)
 
 

time: 160 us -> 159 us (level)
  no operation moved by 1% of the time
where the time goes in v6:
time: 159 us; the launch traced here: 158 us
  Pallas kernels  155 us (97%)
  other arithmetic  2.68 us (2%)
    pallas_call x1, Pallas kernels, per_device(): pl.pallas_call(kernel, out_shape=jax.ShapeDtypeStruct((64, 8192), BF), in...  155 us

profile of v6, /device:TPU:16, one launch (start us, length us, event | category | flops | bytes accessed | tf_op | source)
XLA Modules:
  0.0 157.9 jit_solution(12260269081626544464)
XLA Ops:
  0.0 155.2 %shard_map.64 = bf16[64,8192]{1,0:T(8,128)(2,1)} custom-call(bf16[512,1024]{1,0:T(8,128)(2,1)} %ham.1, bf16[512,1024]{1,0:T(8,128)(2,1)} %den.1, s32[8,16]{1,0:T(8,128)} %h_flags.1, s32[8,16]{1,0:T(8,128)} %p_flags.1, s32[8,16]{1,0:T(8,128)} %q_flags.1, s32[8,16]{1,0:T(8,128)} %r_flags.1), custom_call_target="tpu_custom_call" | custom-call | flops 17179869184 | bytes 4194304 | tf_op jit(solution)/shard_map/pallas_call | solution.py:451
  155.3 2.7 %convert_element_type.3 = f32[64,8192]{1,0:T(8,128)} convert(bf16[64,8192]{1,0:T(8,128)(2,1)} %shard_map.64) | non-fusion elementwise | flops 524288 | bytes 3145728 | tf_op jit(solution)/shard_map/convert_element_type | solution.py:480

commit v7 on v6

--- a/solution.py
+++ b/solution.py
@@ -359,7 +359,7 @@
                 qmask[c, pl.ds(i * B, B), :] = jnp.broadcast_to(q_wide[i : i + 1], (B, T)).astype(BF)
                 rmask[c, pl.ds(i * B, B), :] = jnp.broadcast_to(r_wide[i : i + 1], (B, T)).astype(BF)
 
-    own(0, 0); own(0, 1)
+    own(0, 0); own(0, 1); turn(0, 1, 0)
     rv[yh] = flags[3]
     q_copies = []
     for side in (0, 1):
@@ -375,56 +375,57 @@
     acc[...] = jnp.zeros_like(acc)
     sums[...] = jnp.zeros_like(sums)
     h_swap()
-    h_start(0); turn(0, 1, 0); turn(0, 0, 0); pass_first(0, 1, 0); turn(0, 1, 1); pass_first(0, 1, 1)
-    turn(0, 1, 2); pass_first(0, 0, 0); turn(0, 0, 1); pass_first(0, 0, 1); turn(0, 0, 2); pass_second(0, 0, 0, 0)
-    pass_second(0, 0, 0, 1); h_pass(0, 0); h_pass(0, 1); turn(0, 1, 3); h_start(1); pass_second(0, 0, 1, 0)
-    pass_second(0, 0, 1, 1); h_end(0); pass_second(0, 1, 0, 0); pass_second(0, 1, 0, 1); pass_second(0, 0, 2, 0)
-    pass_second(0, 0, 2, 1); pass_second(0, 1, 1, 0); pass_second(0, 1, 1, 1); pass_second(0, 1, 2, 0)
-    pass_second(0, 1, 2, 1); h_pass(1, 0); own(1, 0); turn(1, 0, 0); h_pass(1, 1); turn(0, 0, 3)
+    h_start(0); turn(0, 0, 0); pass_first(0, 1, 0); turn(0, 1, 1); pass_first(0, 1, 1); turn(0, 1, 2)
+    pass_first(0, 0, 0); pass_first(0, 0, 1); turn(0, 0, 1); turn(0, 0, 2); pass_second(0, 1, 0, 0)
+    pass_second(0, 1, 0, 1); pass_second(0, 0, 0, 0); pass_second(0, 0, 0, 1); h_pass(0, 0); h_pass(0, 1)
+    turn(0, 1, 3); pass_second(0, 0, 1, 0); pass_second(0, 0, 1, 1); h_end(0); h_start(1); pass_second(0, 0, 2, 0)
+    pass_second(0, 0, 2, 1); pass_second(0, 1, 1, 0); pass_second(0, 1, 1, 1); own(1, 0); turn(1, 0, 0)
+    pass_second(0, 1, 2, 0); pass_second(0, 1, 2, 1); own(1, 1); turn(1, 1, 0); turn(0, 0, 3)
     masks()
-    pass_second(1, 0, 0, 0); pass_second(1, 0, 0, 1); pass_second(0, 1, 3, 0); pass_second(0, 1, 3, 1); h_end(1)
-    own(1, 1); turn(1, 1, 0); pass_second(0, 0, 3, 0); pass_second(0, 0, 3, 1)
+    h_pass(1, 0); h_pass(1, 1); pass_second(1, 0, 0, 0); pass_second(1, 0, 0, 1); pass_first(1, 1, 0)
+    turn(1, 1, 1); pass_first(1, 1, 1); turn(1, 1, 2); pass_second(0, 1, 3, 0); pass_second(0, 1, 3, 1); own(2, 0)
+    turn(2, 0, 0); pass_second(0, 0, 3, 0); pass_second(0, 0, 3, 1); pass_first(1, 0, 0); pass_first(1, 0, 1)
+    turn(1, 0, 1); turn(1, 0, 2); h_end(1); turn(1, 1, 3); pass_second(1, 1, 0, 0); pass_second(1, 1, 0, 1)
+    pass_second(2, 0, 0, 0); pass_second(2, 0, 0, 1)
     multiply(0, 0)
     multiply(0, 1)
+    pass_second(1, 1, 1, 0); pass_second(1, 1, 1, 1)
     multiply(0, 2)
-    pass_first(1, 1, 0); turn(1, 1, 1); pass_first(1, 1, 1); turn(1, 1, 2); pass_first(1, 0, 0); turn(1, 0, 1)
-    pass_first(1, 0, 1); turn(1, 0, 2)
     multiply(0, 3)
+    pass_second(1, 0, 1, 0); pass_second(1, 0, 1, 1); pass_second(1, 1, 2, 0); pass_second(1, 1, 2, 1)
+    multiply(1, 0)
+    own(2, 1)
     multiply(0, 4)
     scatter(0)
-    turn(1, 1, 3); pass_second(1, 1, 0, 0); pass_second(1, 1, 0, 1)
-    multiply(1, 0)
-    pass_second(1, 0, 1, 0); pass_second(1, 0, 1, 1); pass_second(1, 1, 1, 0); pass_second(1, 1, 1, 1)
-    pass_second(1, 0, 2, 0); pass_second(1, 0, 2, 1); pass_second(1, 1, 2, 0); pass_second(1, 1, 2, 1)
-    turn(1, 0, 3); own(2, 0); turn(2, 0, 0); ring_start(0); own(2, 1); pass_second(1, 0, 3, 0)
-    pass_second(1, 1, 3, 0); pass_second(1, 1, 3, 1); pass_second(1, 0, 3, 1); turn(2, 1, 0)
+    pass_second(1, 0, 2, 0); pass_second(1, 0, 2, 1); pass_first(2, 0, 0); turn(2, 0, 1); pass_first(2, 0, 1)
+    turn(2, 0, 2); turn(2, 1, 0); turn(1, 0, 3); pass_first(2, 1, 0); turn(2, 1, 1); pass_second(1, 1, 3, 0)
+    pass_second(1, 1, 3, 1); pass_first(2, 1, 1); turn(2, 1, 2)
     multiply(1, 1)
     multiply(1, 2)
-    pass_second(2, 0, 0, 0); pass_second(2, 0, 0, 1)
+    pass_second(2, 0, 1, 0); pass_second(2, 0, 1, 1); turn(2, 0, 3); ring_start(0); pass_second(2, 0, 2, 0)
+    pass_second(2, 0, 2, 1); pass_second(2, 1, 0, 0); pass_second(2, 1, 0, 1)
+    multiply(2, 0)
+    pass_second(1, 0, 3, 0); pass_second(1, 0, 3, 1)
     multiply(1, 3)
-    pass_first(2, 1, 0); turn(2, 1, 1); pass_first(2, 1, 1); turn(2, 1, 2); pass_first(2, 0, 0); turn(2, 0, 1)
-    pass_first(2, 0, 1); turn(2, 0, 2)
+    turn(2, 1, 3); pass_second(2, 1, 1, 0); pass_second(2, 1, 1, 1); pass_second(2, 0, 3, 0)
+    pass_second(2, 0, 3, 1); pass_second(2, 1, 2, 0); pass_second(2, 1, 2, 1)
+    multiply(2, 1)
+    multiply(2, 2)
     multiply(1, 4)
     scatter(1)
-    turn(2, 1, 3); pass_second(2, 1, 0, 0); pass_second(2, 1, 0, 1)
-    multiply(2, 0)
-    pass_second(2, 0, 1, 0); ring_pass(0, 0); ring_pass(0, 1); pass_second(2, 0, 1, 1)
+    pass_second(2, 1, 3, 0); pass_second(2, 1, 3, 1); ring_pass(0, 0); ring_pass(0, 1)
     second(0, 0)
-    pass_second(2, 1, 1, 0); pass_second(2, 1, 1, 1); pass_second(2, 0, 2, 0); pass_second(2, 0, 2, 1)
-    pass_second(2, 1, 2, 0); pass_second(2, 1, 2, 1); turn(2, 0, 3); ring_end(0); ring_start(1)
-    pass_second(2, 1, 3, 0); pass_second(2, 1, 3, 1); pass_second(2, 0, 3, 0); pass_second(2, 0, 3, 1)
-    multiply(2, 1)
-    multiply(2, 2)
-    second(0, 1)
     multiply(2, 3)
     multiply(2, 4)
     scatter(2)
+    ring_start(1); ring_end(0); ring_start(2)
+    second(0, 1)
     second(0, 2)
-    ring_pass(1, 0); ring_pass(1, 1)
+    ring_pass(1, 1); ring_pass(1, 0)
     finish(0)
-    ring_start(2); ring_end(1); ring_pass(2, 0); ring_pass(2, 1)
+    ring_pass(2, 0); ring_pass(2, 1)
     second(1, 0)
-    ring_end(2)
+    ring_end(1); ring_end(2)
     second(1, 1)
     finish(1)
 

time: 159 us -> 158 us (level)
  Pallas kernels: 155 us -> 153 us
    pallas_call x1, Pallas kernels: 155 us -> 153 us  [per_device(): pl.pallas_call(kernel, out_shape=jax.ShapeDtypeStruct((64, 8192), BF), in...]
where the time goes in v7:
time: 158 us; the launch traced here: 156 us
  Pallas kernels  153 us (97%)
  other arithmetic  2.68 us (2%)
    pallas_call x1, Pallas kernels, per_device(): pl.pallas_call(kernel, out_shape=jax.ShapeDtypeStruct((64, 8192), BF), in...  153 us

profile of v7, /device:TPU:16, one launch (start us, length us, event | category | flops | bytes accessed | tf_op | source)
XLA Modules:
  0.0 155.7 jit_solution(7800332609154907091)
XLA Ops:
  0.0 153.0 %shard_map.64 = bf16[64,8192]{1,0:T(8,128)(2,1)} custom-call(bf16[512,1024]{1,0:T(8,128)(2,1)} %ham.1, bf16[512,1024]{1,0:T(8,128)(2,1)} %den.1, s32[8,16]{1,0:T(8,128)} %h_flags.1, s32[8,16]{1,0:T(8,128)} %p_flags.1, s32[8,16]{1,0:T(8,128)} %q_flags.1, s32[8,16]{1,0:T(8,128)} %r_flags.1), custom_call_target="tpu_custom_call" | custom-call | flops 17179869184 | bytes 4194304 | tf_op jit(solution)/shard_map/pallas_call | solution.py:452
  153.0 2.7 %convert_element_type.3 = f32[64,8192]{1,0:T(8,128)} convert(bf16[64,8192]{1,0:T(8,128)(2,1)} %shard_map.64) | non-fusion elementwise | flops 524288 | bytes 3145728 | tf_op jit(solution)/shard_map/convert_element_type | solution.py:481
